TPU v7x, 32 devices: a whole 2x2x4 slice. The times are simulated.
32 devices in a mesh: occ: 16 (over z, y, x), vir: 2 (over core).
Axes of the slice: x: 2, y: 2, z: 4, core: 2. Of those that a mesh axis runs over, the one named last changes fastest.
Arguments:
- t2_tiles: float32 [16, 2, 4, 128, 256], P('occ', 'vir'), may hold values from -6 to 6
- cycle_ints: float32 [16, 2, 4, 256, 128], P('occ', 'vir'), may hold values from -0.21875 to 0.21875
- cycle_left: int32 [16, 2, 24], P('occ', 'vir'), may hold values from 0 to 3
- cycle_right: int32 [16, 2, 24], P('occ', 'vir'), may hold values from 0 to 3
- cycle_dest: int32 [16, 2, 24], P('occ', 'vir'), may hold values from 0 to 31, as said below
- lam_ladder: float32 [4096, 1024], P('occ', 'vir'), may hold values from -6 to 6
- ladder_ints: float32 [1024, 256], P('vir'), may hold values from -0.1875 to 0.1875
- ladder_mask: int32 [32, 8], P('occ', 'vir'), may hold values 0 or 1
- partner_slot: int32 [16, 2], P('occ'), may hold values from 0 to 1, as said below
- denom: float32 [4096, 256], P('occ', 'vir'), may hold values from 1 to 8
Outputs:
- increment: float32 [4096, 256], P('occ', 'vir')
Inputs may be any that keep to these rules, and one draw needn't show every extreme that they name: One device's tasks name each owner (cycle_dest // 2) at most 3 times; in each vir column one owner is named exactly 3 times by every device. `partner_slot`: each row is a permutation of the 2 slots.
All inputs are finite; a program needn't handle non-finite values. No bound on the sum of `ladder_mask` on one device may be relied on, other than what follows from the above.
Results may differ from a plain program's by a relative error of at most 0.0001.
Values sent between devices are 32-bit elements; how exact they have to be, the bound alone decides.
A program may use at most 128 MiB of HBM per device.

v0:
```python
import jax
import jax.numpy as jnp
from jax import lax
from jax.sharding import PartitionSpec as P

CAP = 3


def partner_2(array, axis, distance):
    return lax.ppermute(array, axis, [(i, i ^ 1 << distance) for i in range(lax.axis_size(axis))])


def body(
    t2_tiles,
    cycle_ints,
    cycle_left,
    cycle_right,
    cycle_dest,
    lam_ladder,
    ladder_ints,
    ladder_mask,
    partner_slot,
    denom,
):
    highest = lax.Precision.HIGHEST
    owned = partner_slot.shape[1]
    edge = denom.shape[1]
    blocks = ladder_mask.shape[1]
    n_occ = lax.axis_size("occ")
    shaped = lam_ladder.reshape(owned, edge, blocks, edge)
    masked = (shaped * ladder_mask.astype(jnp.float32)[:, None, :, None]).reshape(
        owned * edge, blocks * edge
    )
    partial_ladder = jnp.dot(masked, ladder_ints, precision=highest)
    ladder = lax.psum_scatter(partial_ladder, "vir", scatter_dimension=1, tiled=True)
    left_tiles = t2_tiles[0, 0]
    right_tiles = cycle_ints[0, 0]
    lefts = cycle_left[0, 0]
    rights = cycle_right[0, 0]
    dests = cycle_dest[0, 0]
    count = dests.shape[0]

    def task_block(pair):
        lidx, ridx = pair
        return jnp.einsum("btk,bkc->btc", left_tiles[lidx], right_tiles[ridx], precision=highest)

    partials = lax.map(task_block, (lefts.reshape(-1, 8), rights.reshape(-1, 8))).reshape(
        count, edge, edge
    )
    owners = dests // owned
    slots = dests % owned
    onehot = (owners[:, None] == jnp.arange(n_occ, dtype=jnp.int32)[None, :]).astype(jnp.int32)
    before = jnp.cumsum(onehot, axis=0) - onehot
    rank = jnp.sum(before * onehot, axis=1)
    position = owners * CAP + rank
    slot_task = (
        jax.ops.segment_sum(
            jnp.arange(count, dtype=jnp.int32) + 1, position, num_segments=n_occ * CAP
        )
        - 1
    )
    valid = slot_task >= 0
    index = jnp.maximum(slot_task, 0)
    send_tiles = (partials[index] * valid.astype(jnp.float32)[:, None, None]).reshape(
        n_occ, CAP, edge, edge
    )
    send_slots = jnp.where(valid, slots[index], owned).reshape(n_occ, CAP)
    got_tiles, got_slots = (
        lax.all_to_all(send_tiles, "occ", split_axis=0, concat_axis=0, tiled=True),
        lax.all_to_all(send_slots, "occ", split_axis=0, concat_axis=0, tiled=True),
    )
    select = (got_slots[:, :, None] == jnp.arange(owned, dtype=jnp.int32)[None, None, :]).astype(
        jnp.float32
    )
    cycle = jnp.einsum("ncij,ncs->sij", got_tiles, select, precision=highest)
    resid = ladder.reshape(owned, edge, edge) + cycle
    moved = resid
    for bit in range(n_occ.bit_length() - 1):
        moved = partner_2(moved, "occ", bit)
    partner = moved[partner_slot[0]][:, ::-1, ::-1]
    sym = (resid + partner).reshape(owned * edge, edge)
    return sym / denom


def solution(mesh):
    in_specs = (
        P("occ", "vir", None, None, None),
        P("occ", "vir", None, None, None),
        P("occ", "vir", None),
        P("occ", "vir", None),
        P("occ", "vir", None),
        P("occ", "vir"),
        P("vir", None),
        P("occ", "vir"),
        P("occ", None),
        P("occ", "vir"),
    )
    out_specs = P("occ", "vir")
    return jax.shard_map(body, mesh=mesh, in_specs=in_specs, out_specs=out_specs, check_vma=False)
```

profile of v0, /device:TPU:0, one launch (start us, length us, event | category | flops | bytes accessed | tf_op | source)
XLA Modules:
  0.0 157.7 jit_solution(6477073773780086828)
XLA Ops:
  6.5 0.7 and_select_fusion
  7.3 0.1 fusion.15
  7.4 0.2 select_reduce_fusion
  7.6 0.7 fusion.21
  8.2 0.7 scatter_custom_fusion
  9.0 0.8 gather_fusion.2
  9.8 0.7 all_to_all.9
  10.4 8.3 %all-to-all-start = ((s32[16,1,3]{2,1,0:T(1,128)}), s32[16,1,3]{2,1,0:T(1,128)S(1)}, u32[]{:S(2)}, u32[]{:S(2)}) async-start(s32[16,1,3]{2,1,0:T(1,128)} %bitcast.10), calls=%async_computation.1 | async-start | bytes 16384 | tf_op jit(solution)/shard_map/all_to_all | solution.py:70
  18.8 0.6 broadcast.227
  19.4 1.3 reduce.6
  20.7 0.1 reshape_squeeze.6
  20.8 1.3 reduce.7
  22.1 0.1 reshape_squeeze.7
  22.1 15.9 %while.10 = (s32[]{:T(128)}, f32[3,8,128,128]{3,2,1,0:T(8,128)}, s32[3,8]{1,0:T(4,128)S(1)}, f32[4,128,256]{2,1,0:T(8,128)}, s32[3,8]{1,0:T(4,128)S(1)}, /*index=5*/f32[4,256,128]{2,1,0:T(8,128)}, s32[]{:T(128)}) while((s32[]{:T(128)}, f32[3,8,128,128]{3,2,1,0:T(8,128)}, s32[3,8]{1,0:T(4,128)S(1)}, f32[4,128,256]{2,1,0:T(8,128)}, ...), condition=%wide.region_5.6_spmd, body=%wide.region_4.5_spmd.sunk | while | flops 402655296 | bytes 6824785 | solution.py:47
  22.2 1.7 %gather_fusion = f32[8,128,256]{2,1,0:T(8,128)S(1)} fusion(f32[4,128,256]{2,1,0:T(8,128)} %get-tuple-element.112, s32[1024]{0:T(1024)S(1)} %pad_clamp_fusion.6), kind=kCustom, calls=%fused_computation.clone.1 | custom fusion | bytes 2097184 | tf_op jit(solution)/shard_map/while/body/eval_jaxpr/gather | solution.py:45
  23.8 1.7 %gather_fusion.1 = f32[8,256,128]{2,1,0:T(8,128)S(1)} fusion(f32[4,256,128]{2,1,0:T(8,128)} %get-tuple-element.114, s32[1024]{0:T(1024)S(1)} %pad_clamp_fusion.7), kind=kCustom, calls=%fused_computation.1.clone.1 | custom fusion | bytes 2097184 | tf_op jit(solution)/shard_map/while/body/eval_jaxpr/gather | solution.py:45
  25.5 1.9 %fusion.34 = f32[3,8,128,128]{3,2,1,0:T(8,128)} fusion(f32[3,8,128,128]{3,2,1,0:T(8,128)} %get-tuple-element.103, s32[]{:T(128)} %get-tuple-element.102, f32[8,128,256]{2,1,0:T(8,128)S(1)} %gather_fusion, f32[8,256,128]{2,1,0:T(8,128)S(1)} %gather_fusion.1), kind=kOutput, calls=%fused_computation.7.clone.1 | convolution fusion | flops 402653184 | bytes 2621952 | tf_op jit(solution)/shard_map/while/body/eval_jaxpr/btk,bkc->btc/dot_general | solution.py:45
  27.5 1.7 %gather_fusion = f32[8,128,256]{2,1,0:T(8,128)S(1)} fusion(f32[4,128,256]{2,1,0:T(8,128)} %get-tuple-element.112, s32[1024]{0:T(1024)S(1)} %pad_clamp_fusion.6), kind=kCustom, calls=%fused_computation.clone.1 | custom fusion | bytes 2097184 | tf_op jit(solution)/shard_map/while/body/eval_jaxpr/gather | solution.py:45
  29.1 1.7 %gather_fusion.1 = f32[8,256,128]{2,1,0:T(8,128)S(1)} fusion(f32[4,256,128]{2,1,0:T(8,128)} %get-tuple-element.114, s32[1024]{0:T(1024)S(1)} %pad_clamp_fusion.7), kind=kCustom, calls=%fused_computation.1.clone.1 | custom fusion | bytes 2097184 | tf_op jit(solution)/shard_map/while/body/eval_jaxpr/gather | solution.py:45
  30.8 2.0 %fusion.34 = f32[3,8,128,128]{3,2,1,0:T(8,128)} fusion(f32[3,8,128,128]{3,2,1,0:T(8,128)} %get-tuple-element.103, s32[]{:T(128)} %get-tuple-element.102, f32[8,128,256]{2,1,0:T(8,128)S(1)} %gather_fusion, f32[8,256,128]{2,1,0:T(8,128)S(1)} %gather_fusion.1), kind=kOutput, calls=%fused_computation.7.clone.1 | convolution fusion | flops 402653184 | bytes 2621952 | tf_op jit(solution)/shard_map/while/body/eval_jaxpr/btk,bkc->btc/dot_general | solution.py:45
  32.8 1.7 %gather_fusion = f32[8,128,256]{2,1,0:T(8,128)S(1)} fusion(f32[4,128,256]{2,1,0:T(8,128)} %get-tuple-element.112, s32[1024]{0:T(1024)S(1)} %pad_clamp_fusion.6), kind=kCustom, calls=%fused_computation.clone.1 | custom fusion | bytes 2097184 | tf_op jit(solution)/shard_map/while/body/eval_jaxpr/gather | solution.py:45
  34.5 1.7 %gather_fusion.1 = f32[8,256,128]{2,1,0:T(8,128)S(1)} fusion(f32[4,256,128]{2,1,0:T(8,128)} %get-tuple-element.114, s32[1024]{0:T(1024)S(1)} %pad_clamp_fusion.7), kind=kCustom, calls=%fused_computation.1.clone.1 | custom fusion | bytes 2097184 | tf_op jit(solution)/shard_map/while/body/eval_jaxpr/gather | solution.py:45
  36.1 2.0 %fusion.34 = f32[3,8,128,128]{3,2,1,0:T(8,128)} fusion(f32[3,8,128,128]{3,2,1,0:T(8,128)} %get-tuple-element.103, s32[]{:T(128)} %get-tuple-element.102, f32[8,128,256]{2,1,0:T(8,128)S(1)} %gather_fusion, f32[8,256,128]{2,1,0:T(8,128)S(1)} %gather_fusion.1), kind=kOutput, calls=%fused_computation.7.clone.1 | convolution fusion | flops 402653184 | bytes 2621952 | tf_op jit(solution)/shard_map/while/body/eval_jaxpr/btk,bkc->btc/dot_general | solution.py:45
  38.1 3.8 %gather_fusion.3 = f32[48,128,128]{2,1,0:T(8,128)} fusion(f32[24,128,128]{2,1,0:T(8,128)} %bitcast.93, s32[1024]{0:T(1024)S(1)} %pad_clamp_fusion.3), kind=kCustom, calls=%fused_computation.3 | custom fusion | bytes 6291648 | tf_op jit(solution)/shard_map/gather | solution.py:64
  41.9 0.1 reshape.201
  42.0 3.8 %broadcast_multiply_fusion = f32[16,3,128,128]{3,2,1,0:T(8,128)} fusion(f32[16,3,128,128]{3,2,1,0:T(8,128)} %bitcast.92, f32[16,3]{1,0:T(8,128)S(1)} %reshape.201), kind=kLoop, calls=%fused_computation.20 | loop fusion | flops 786432 | bytes 6291648 | tf_op jit(solution)/shard_map/mul | solution.py:64
  45.8 7.1 %all-to-all-start.1 = ((f32[16,3,128,128]{3,2,1,0:T(8,128)}), f32[16,3,128,128]{3,2,1,0:T(8,128)}, u32[]{:S(2)}, u32[]{:S(2)}) async-start(f32[16,3,128,128]{3,2,1,0:T(8,128)} %broadcast_multiply_fusion), calls=%async_computation.2 | async-start | bytes 6291456 | tf_op jit(solution)/shard_map/all_to_all | solution.py:69
  52.9 0.0 reduce-scatter.2.cloned.1.call-start
  53.0 0.1 mul.37
  53.2 1.3 fusion.13
  54.5 0.0 reduce-scatter.2.cloned.1.call-update
  54.5 0.1 copy.30
  54.6 10.3 %reduce-scatter.2.cloned.1.call-done = f32[256,128]{1,0:T(8,128)} async-done(((f32[256,256]{1,0:T(8,128)}), f32[256,128]{1,0:T(8,128)}) %reduce-scatter.2.cloned.1.call-update) | async-done | bytes 131088 | tf_op jit(solution)/shard_map/reduce_scatter | solution.py:35
  65.0 48.8 %all-to-all-done.1 = f32[16,3,128,128]{3,2,1,0:T(8,128)} async-done(((f32[16,3,128,128]{3,2,1,0:T(8,128)}), f32[16,3,128,128]{3,2,1,0:T(8,128)}, u32[]{:S(2)}, u32[]{:S(2)}) %all-to-all-start.1) | async-done | bytes 3145760 | tf_op jit(solution)/shard_map/all_to_all | solution.py:69
  113.8 4.7 %fusion.10 = f32[2,128,128]{2,0,1:T(2,128)S(1)} fusion(f32[16,3,128,128]{3,2,1,0:T(8,128)} %all-to-all-done.1, f32[2,128,128]{2,1,0:T(8,128)} %bitcast.95, s32[16,3]{0,1:T(4,128)S(1)} %bitcast.96), kind=kOutput, calls=%fused_computation.22 | convolution fusion | flops 18907232 | bytes 3408064 | tf_op jit(solution)/shard_map/ncij,ncs->sij/dot_general | solution.py:75
  118.5 1.3 collective-permute-start
  119.7 3.8 %collective-permute-done = f32[2,128,128]{2,0,1:T(2,128)S(1)} collective-permute-done((f32[2,128,128]{2,0,1:T(2,128)S(1)}, f32[2,128,128]{2,0,1:T(2,128)S(1)}, u32[]{:S(2)}, u32[]{:S(2)}) %collective-permute-start) | collective-permute-done | bytes 131104 | tf_op jit(solution)/shard_map/ppermute | solution.py:10
  123.5 4.7 %collective-permute-start.1 = (f32[2,128,128]{2,0,1:T(2,128)S(1)}, f32[2,128,128]{2,0,1:T(2,128)S(1)}, u32[]{:S(2)}, u32[]{:S(2)}) collective-permute-start(f32[2,128,128]{2,0,1:T(2,128)S(1)} %collective-permute-done), channel_id=1, source_target_pairs={{0,4},{2,6},{4,0},{6,2},{8,12},{10,14},{12,8},{14,10},{16,20},{18,... | collective-permute-start | bytes 393224 | tf_op jit(solution)/shard_map/ppermute | solution.py:10
  128.2 2.9 %collective-permute-done.1 = f32[2,128,128]{2,0,1:T(2,128)S(1)} collective-permute-done((f32[2,128,128]{2,0,1:T(2,128)S(1)}, f32[2,128,128]{2,0,1:T(2,128)S(1)}, u32[]{:S(2)}, u32[]{:S(2)}) %collective-permute-start.1) | collective-permute-done | bytes 131104 | tf_op jit(solution)/shard_map/ppermute | solution.py:10
  131.1 7.9 %collective-permute-start.2 = (f32[2,128,128]{2,0,1:T(2,128)S(1)}, f32[2,128,128]{2,0,1:T(2,128)S(1)}, u32[]{:S(2)}, u32[]{:S(2)}) collective-permute-start(f32[2,128,128]{2,0,1:T(2,128)S(1)} %collective-permute-done.1), channel_id=1, source_target_pairs={{0,8},{2,10},{4,12},{6,14},{8,0},{10,2},{12,4},{14,6},{16,24},{18,... | collective-permute-start | bytes 393224 | tf_op jit(solution)/shard_map/ppermute | solution.py:10
  139.0 4.2 %collective-permute-done.2 = f32[2,128,128]{2,0,1:T(2,128)S(1)} collective-permute-done((f32[2,128,128]{2,0,1:T(2,128)S(1)}, f32[2,128,128]{2,0,1:T(2,128)S(1)}, u32[]{:S(2)}, u32[]{:S(2)}) %collective-permute-start.2) | collective-permute-done | bytes 131104 | tf_op jit(solution)/shard_map/ppermute | solution.py:10
  143.2 3.0 %collective-permute-start.3 = (f32[2,128,128]{2,0,1:T(2,128)S(1)}, f32[2,128,128]{2,0,1:T(2,128)S(1)}, u32[]{:S(2)}, u32[]{:S(2)}) collective-permute-start(f32[2,128,128]{2,0,1:T(2,128)S(1)} %collective-permute-done.2), channel_id=1, source_target_pairs={{0,16},{2,18},{4,20},{6,22},{8,24},{10,26},{12,28},{14,30},{16,0},... | collective-permute-start | bytes 393224 | tf_op jit(solution)/shard_map/ppermute | solution.py:10
  146.2 2.9 %collective-permute-done.3 = f32[2,128,128]{2,0,1:T(2,128)S(1)} collective-permute-done((f32[2,128,128]{2,0,1:T(2,128)S(1)}, f32[2,128,128]{2,0,1:T(2,128)S(1)}, u32[]{:S(2)}, u32[]{:S(2)}) %collective-permute-start.3) | collective-permute-done | bytes 131104 | tf_op jit(solution)/shard_map/ppermute | solution.py:10
  149.1 0.6 gather_fusion.4
  149.7 0.1 copy.34
  149.8 0.3 rev.3
  150.1 0.1 add.83
  150.2 0.7 bitcast_divide_fusion
  (32 shorter events, 0.2 us)
Async XLA Ops:
  6.5 46.6 %copy-start = (f32[512,256]{1,0:T(8,128)S(1)}, f32[512,256]{1,0:T(8,128)}, u32[]{:S(2)}) copy-start(f32[512,256]{1,0:T(8,128)} %param.18) | copy-start | bytes 1572868
  10.4 35.4 %all-to-all-start = ((s32[16,1,3]{2,1,0:T(1,128)}), s32[16,1,3]{2,1,0:T(1,128)S(1)}, u32[]{:S(2)}, u32[]{:S(2)}) async-start(s32[16,1,3]{2,1,0:T(1,128)} %bitcast.10), calls=%async_computation.1 | async-start | bytes 16384 | tf_op jit(solution)/shard_map/all_to_all | solution.py:70
  45.8 7.2 %copy-start.3 = (s32[2,4]{1,0:T(2,128)S(1)}, s32[2,4]{1,0:T(2,128)}, u32[]{:S(2)}) copy-start(s32[2,4]{1,0:T(2,128)} %param.19) | copy-start | bytes 100
  45.8 7.3 %copy-start.1 = (f32[256,512]{1,0:T(8,128)S(1)}, f32[256,512]{1,0:T(8,128)}, u32[]{:S(2)}) copy-start(f32[256,512]{1,0:T(8,128)} %param.17) | copy-start | bytes 1572868
  45.8 67.9 %all-to-all-start.1 = ((f32[16,3,128,128]{3,2,1,0:T(8,128)}), f32[16,3,128,128]{3,2,1,0:T(8,128)}, u32[]{:S(2)}, u32[]{:S(2)}) async-start(f32[16,3,128,128]{3,2,1,0:T(8,128)} %broadcast_multiply_fusion), calls=%async_computation.2 | async-start | bytes 6291456 | tf_op jit(solution)/shard_map/all_to_all | solution.py:69
  52.9 93.3 %copy-start.4 = (s32[1,2]{1,0:T(1,128)S(1)}, s32[1,2]{1,0:T(1,128)}, u32[]{:S(2)}) copy-start(s32[1,2]{1,0:T(1,128)} %param.20) | copy-start | bytes 28
  52.9 12.0 %reduce-scatter.2.cloned.1.call-start = ((), (), s32[]{:S(2)}) async-start(), calls=%async_computation.3 | async-start | bytes 393216 | tf_op jit(solution)/shard_map/reduce_scatter | solution.py:35
  54.5 95.7 %copy-start.2 = (f32[256,128]{1,0:T(8,128)S(1)}, f32[256,128]{1,0:T(8,128)}, u32[]{:S(2)}) copy-start(f32[256,128]{1,0:T(8,128)} %param.21) | copy-start | bytes 393220
  118.5 5.0 %collective-permute-start = (f32[2,128,128]{2,0,1:T(2,128)S(1)}, f32[2,128,128]{2,0,1:T(2,128)S(1)}, u32[]{:S(2)}, u32[]{:S(2)}) collective-permute-start(f32[2,128,128]{2,0,1:T(2,128)S(1)} %fusion.10), channel_id=1, source_target_pairs={{0,2},{2,0},{4,6},{6,4},{8,10},{10,8},{12,14},{14,12},{16,18},{18,... | collective-permute-start | bytes 393224 | tf_op jit(solution)/shard_map/ppermute | solution.py:10
  123.5 7.6 %collective-permute-start.1 = (f32[2,128,128]{2,0,1:T(2,128)S(1)}, f32[2,128,128]{2,0,1:T(2,128)S(1)}, u32[]{:S(2)}, u32[]{:S(2)}) collective-permute-start(f32[2,128,128]{2,0,1:T(2,128)S(1)} %collective-permute-done), channel_id=1, source_target_pairs={{0,4},{2,6},{4,0},{6,2},{8,12},{10,14},{12,8},{14,10},{16,20},{18,... | collective-permute-start | bytes 393224 | tf_op jit(solution)/shard_map/ppermute | solution.py:10
  131.1 12.1 %collective-permute-start.2 = (f32[2,128,128]{2,0,1:T(2,128)S(1)}, f32[2,128,128]{2,0,1:T(2,128)S(1)}, u32[]{:S(2)}, u32[]{:S(2)}) collective-permute-start(f32[2,128,128]{2,0,1:T(2,128)S(1)} %collective-permute-done.1), channel_id=1, source_target_pairs={{0,8},{2,10},{4,12},{6,14},{8,0},{10,2},{12,4},{14,6},{16,24},{18,... | collective-permute-start | bytes 393224 | tf_op jit(solution)/shard_map/ppermute | solution.py:10
  143.2 5.9 %collective-permute-start.3 = (f32[2,128,128]{2,0,1:T(2,128)S(1)}, f32[2,128,128]{2,0,1:T(2,128)S(1)}, u32[]{:S(2)}, u32[]{:S(2)}) collective-permute-start(f32[2,128,128]{2,0,1:T(2,128)S(1)} %collective-permute-done.2), channel_id=1, source_target_pairs={{0,16},{2,18},{4,20},{6,22},{8,24},{10,26},{12,28},{14,30},{16,0},... | collective-permute-start | bytes 393224 | tf_op jit(solution)/shard_map/ppermute | solution.py:10
Sparse Core Ops, SparseCore 0:
  56.0 8.9 reduce-scatter.1
where the time goes:
time: 159 us; the launch traced here: 158 us
  waiting for transfers between devices  73 us (46%)
  starting transfers between devices  32.3 us (20%)
  local copies, waits for them, and re-layouts  17.3 us (11%)
  between operations  13.5 us (8%)
  matrix products  11.9 us (7%)
  other arithmetic  9.71 us (6%)
    all_to_all x1, waiting for transfers between devices, body(): lax.all_to_all(send_tiles, 'occ', split_axis=0, concat_axis=0, tiled=True)  48.8 us
    ppermute x4, starting transfers between devices, partner_2(): lax.ppermute(array, axis, [(i, i ^ 1 << distance) for i in range(lax.axis...  16.8 us
    ppermute x4, waiting for transfers between devices, partner_2(): lax.ppermute(array, axis, [(i, i ^ 1 << distance) for i in range(lax.axis...  13.8 us
    reduce_scatter x1, waiting for transfers between devices, body(): lax.psum_scatter(partial_ladder, 'vir', scatter_dimension=1, tiled=True)  10.3 us
    all_to_all x1, starting transfers between devices, body(): lax.all_to_all(send_slots, 'occ', split_axis=0, concat_axis=0, tiled=True)  8.31 us
    all_to_all x1, starting transfers between devices, body(): lax.all_to_all(send_tiles, 'occ', split_axis=0, concat_axis=0, tiled=True)  7.09 us
    dot_general x3, matrix products, task_block(): jnp.einsum('btk,bkc->btc', left_tiles[lidx], right_tiles[ridx], precision...  5.86 us
    gather x3, local copies, waits for them, and re-layouts, task_block(): right_tiles[ridx]  4.97 us
  transfers between devices with their start and end apart: 7, of which 6 were waited for; matrix products, arithmetic and copies ran while one was open for 18% of the time, Pallas kernels for 0%

commit v1 on v0

v1 whole, which is shorter than its diff:
```python
import functools

import jax
import jax.numpy as jnp
from jax import lax
from jax.experimental import pallas as pl
from jax.experimental.pallas import tpu as pltpu
from jax.sharding import PartitionSpec as P

CAP = 3
MESH = pl.DeviceIdType.MESH
f32 = jnp.float32
bf16 = jnp.bfloat16


def split2(x):
    hi = x.astype(bf16)
    return hi, (x - hi.astype(f32)).astype(bf16)


def dot(a, b):
    return jnp.dot(a, b, preferred_element_type=f32)


def dot3(a, b):
    return dot(a[0], b[0]) + (dot(a[0], b[1]) + dot(a[1], b[0]))


def toggle(value, bit, on=1):
    return value + on * bit * (1 - 2 * ((value // bit) % 2))


def chunk_plan(edge):
    unit = edge // 2 // 8
    big = unit // 3 + unit % 3 // 2
    sizes = [big * 8, big * 8, (unit - 2 * big) * 8]
    return [(sum(sizes[:c]), sizes[c]) for c in range(3)]


def kernel(
    n_occ, n_vir, chunks,
    left, right, dest, mask, slot, t2_hbm, ints_hbm, lam_hbm, lints_hbm,
    out,
    t2, ints, lam, lints, code_v, code_s, prod, lam_hi, lam_lo, lad, lad_got, flag, flag_got,
    c0, c1, c2, r0, r1, r2, s0, s1, s2, t0, t1, t2s, g0, g1, g2, w0, w1, w2,
    load_sem, code_sem, send_sem, recv_sem, fin_send, fin_recv, lad_send, lad_recv, flag_send, flag_recv,
):
    acc, got, own, fin, fin_got, flips = (c0, c1, c2), (r0, r1, r2), (s0, s1, s2), (t0, t1, t2s), (g0, g1, g2), (w0, w1, w2)
    edge = prod.shape[1]
    xt = t2.shape[0]
    owned = 2
    count = dest.shape[2]
    bits = n_occ.bit_length() - 1
    levels = bits - 1
    blocks = n_occ // 2
    width = (xt * xt).bit_length()
    p = lax.axis_index("occ")
    q = lax.axis_index("vir")
    upper = p // blocks
    cls = p + upper * (n_occ - 1 - 2 * p)
    partner = n_occ - 1 - p
    orders = [[1 << ((c + levels - 1 - h) % levels) for h in range(levels)] for c in range(3)]

    loads = [
        pltpu.make_async_copy(src, dst, load_sem.at[i])
        for i, (src, dst) in enumerate(
            ((t2_hbm.at[0, 0], t2), (ints_hbm.at[0, 0], ints), (lam_hbm, lam), (lints_hbm, lints))
        )
    ]
    for load in loads:
        load.start()

    barrier = pltpu.get_barrier_semaphore()
    for b in range(levels):
        pl.semaphore_signal(barrier, inc=1, device_id=(toggle(p, 1 << b), q), device_id_type=MESH)
    pl.semaphore_signal(barrier, inc=1, device_id=(partner, q), device_id_type=MESH)
    for off in range(1, n_vir):
        pl.semaphore_signal(barrier, inc=1, device_id=(p, (q + off) % n_vir), device_id_type=MESH)

    tile_id = lax.broadcasted_iota(jnp.int32, code_v.shape, 0) * 128 + lax.broadcasted_iota(
        jnp.int32, code_v.shape, 1
    )

    def note(t, packed):
        code = left[0, 0, t] * xt + right[0, 0, t] + 1
        return jnp.where(tile_id == dest[0, 0, t], packed * (1 << width) + code, packed)

    code_v[...] = lax.fori_loop(0, count, note, jnp.zeros(code_v.shape, jnp.int32))
    codes = pltpu.make_async_copy(code_v, code_s, code_sem)
    codes.start()
    flag[...] = jnp.full(flag.shape, slot[0, 0], jnp.int32)
    prod[0] = jnp.zeros((edge, edge), f32)

    loads[0].wait()
    loads[1].wait()
    a = split2(t2[...].reshape(xt * edge, t2.shape[2]))
    for r in range(0, xt, 2):
        b = split2(jnp.concatenate([ints[r], ints[r + 1]], axis=1))
        res = dot3(a, b)
        for l in range(xt):
            for d in range(2):
                prod[1 + l * xt + r + d] = res[l * edge : (l + 1) * edge, d * edge : (d + 1) * edge]
    codes.wait()

    def assemble(c, i):
        lo, half = chunks[c]
        home = cls
        for h in range(levels):
            home = toggle(home, orders[c][h], (i // (1 << h)) % 2)
        for j in range(2 * owned):
            owner = home if j < owned else n_occ - 1 - home
            g = owner * owned + j % owned
            packed = code_s[g // 128, g % 128]
            ids = [lax.shift_right_logical(packed, width * k) & ((1 << width) - 1) for k in range(CAP)]
            for at, row in ((0, lo), (half, edge - lo - half)):
                tiles = [prod[k, row : row + half, :] for k in ids]
                acc[c][i, j, at : at + half, :] = tiles[0] + tiles[1] + tiles[2]

    def step_copy(c, i, h):
        return pltpu.make_async_remote_copy(
            src_ref=acc[c].at[i],
            dst_ref=got[c].at[i],
            send_sem=send_sem.at[c, i],
            recv_sem=recv_sem.at[c, i],
            device_id=(toggle(p, orders[c][h]), q),
            device_id_type=MESH,
        )

    pl.semaphore_wait(barrier, bits + n_vir - 1)
    flag_copy = pltpu.make_async_remote_copy(
        src_ref=flag, dst_ref=flag_got, send_sem=flag_send, recv_sem=flag_recv,
        device_id=(partner, q), device_id_type=MESH,
    )
    flag_copy.start()

    top = blocks // 2

    @pl.loop(0, top)
    def _(n):
        i = blocks - 1 - n
        for c in range(3):
            assemble(c, i)
            step_copy(c, i, levels - 1).start()

    @pl.loop(0, top)
    def _(n):
        for c in range(3):
            assemble(c, top - 1 - n)

    loads[2].wait()
    loads[3].wait()
    for s in range(owned):
        for b in range(mask.shape[1]):
            rows, cols = pl.ds(s * edge, edge), pl.ds(b * edge, edge)
            hi, lo = split2(lam[rows, cols] * mask[s, b].astype(f32))
            lam_hi[rows, cols] = hi
            lam_lo[rows, cols] = lo

    def ladder(column):
        cols = pl.ds(pl.multiple_of(column * edge, edge), edge)
        return dot3((lam_hi[...], lam_lo[...]), split2(lints[:, cols]))

    lad_copies = []
    for off in range(1, n_vir):
        column = (q + off) % n_vir
        lad[off] = ladder(column)
        lad_copies.append(
            pltpu.make_async_remote_copy(
                src_ref=lad.at[off], dst_ref=lad_got.at[off - 1],
                send_sem=lad_send.at[off - 1], recv_sem=lad_recv.at[off - 1],
                device_id=(p, column), device_id_type=MESH,
            )
        )
        lad_copies[-1].start()
    lad[0] = ladder(q)

    def take(c, i, h):
        for k in range(h, levels):
            step_copy(c, i + (1 << k), k).wait_recv()
            acc[c][i] = acc[c][i] + got[c][i + (1 << k)]

    for h in reversed(range(levels - 1)):

        @pl.loop(0, 1 << h)
        def _(n):
            i = 2 * (1 << h) - 1 - n
            for c in range(3):
                take(c, i, h + 1)
                step_copy(c, i, h).start()

    for copy in lad_copies:
        copy.wait_recv()
    total = lad[0]
    for off in range(1, n_vir):
        total = total + lad_got[off - 1]
    lad[0] = total
    flag_copy.wait_recv()
    lanes = lax.broadcasted_iota(jnp.int32, (edge, edge), 0) + lax.broadcasted_iota(jnp.int32, (edge, edge), 1)
    turn_lanes = jnp.where(lanes == edge - 1, 1.0, 0.0).astype(bf16)

    def fin_copy(c):
        return pltpu.make_async_remote_copy(
            src_ref=fin[c], dst_ref=fin_got[c], send_sem=fin_send.at[c], recv_sem=fin_recv.at[c],
            device_id=(partner, q), device_id_type=MESH,
        )

    for c in range(3):
        lo, half = chunks[c]
        m = 2 * half
        take(c, 0, 0)
        for s in range(owned):
            j = upper * owned + s
            for at, row in ((0, lo), (half, edge - lo - half)):
                here = pl.ds(at, half)
                acc[c][0, j, here, :] = acc[c][0, j, here, :] + lad[0, s * edge + row : s * edge + row + half, :]
        x = acc[c][0].reshape(4 * m, edge)
        hi, rest = split2(x)
        mid, low = split2(x - hi.astype(f32))
        size = 4 * m
        rows = lax.broadcasted_iota(jnp.int32, (size, size), 0) + lax.broadcasted_iota(jnp.int32, (size, size), 1)
        turn_rows = jnp.where(rows == size - 1, 1.0, 0.0).astype(bf16)
        y = None
        for piece in (hi, mid, low):
            part = dot(turn_rows, dot(piece, turn_lanes).astype(bf16))
            y = part if y is None else y + part
        flips[c][...] = y.reshape(4, m, edge)
        for target, which, swap in ((fin[c], 1 - upper, flag_got), (own[c], upper, flag)):
            first = flips[c][2 * which + 1]
            second = flips[c][2 * which]
            keep = jnp.broadcast_to(swap[0:1, :] == 0, (m, edge))
            target[0] = acc[c][0, 2 * which] + jnp.where(keep, first, second)
            target[1] = acc[c][0, 2 * which + 1] + jnp.where(keep, second, first)
            if target is fin[c]:
                fin_copy(c).start()

    for c in range(3):
        lo, half = chunks[c]
        fin_copy(c).wait_recv()
        for s in range(owned):
            for at, row in ((0, lo), (half, edge - lo - half)):
                out[s * edge + row : s * edge + row + half, :] = (
                    own[c][s, at : at + half, :] + fin_got[c][s, at : at + half, :]
                )

    flag_copy.wait_send()
    for copy in lad_copies:
        copy.wait_send()
    for c in range(3):
        fin_copy(c).wait_send()
        for h in range(levels):

            @pl.loop(1 << h, 2 << h)
            def _(i):
                step_copy(c, i, h).wait_send()


def body(
    n_occ, n_vir,
    t2_tiles, cycle_ints, cycle_left, cycle_right, cycle_dest, lam_ladder, ladder_ints, ladder_mask, partner_slot, denom,
):
    edge = denom.shape[1]
    owned = partner_slot.shape[1]
    xt, kc = cycle_ints.shape[2], cycle_ints.shape[3]
    blocks = n_occ // 2
    chunks = chunk_plan(edge)
    tiles = n_occ * owned
    code_rows = -(-tiles // 128)
    rows = owned * edge
    per_chunk = lambda *lead: [pltpu.VMEM((*lead, 2 * half, edge), f32) for _, half in chunks]
    sem = pltpu.SemaphoreType.DMA
    smem = pl.BlockSpec(memory_space=pltpu.SMEM)
    hbm = pl.BlockSpec(memory_space=pl.ANY)
    sym = pl.pallas_call(
        functools.partial(kernel, n_occ, n_vir, chunks),
        out_shape=jax.ShapeDtypeStruct((rows, edge), f32),
        in_specs=[smem] * 5 + [hbm] * 4,
        out_specs=pl.BlockSpec(memory_space=pltpu.VMEM),
        scratch_shapes=[
            pltpu.VMEM((xt, edge, kc), f32),
            pltpu.VMEM((xt, kc, edge), f32),
            pltpu.VMEM(lam_ladder.shape, f32),
            pltpu.VMEM(ladder_ints.shape, f32),
            pltpu.VMEM((code_rows, 128), jnp.int32),
            pltpu.SMEM((code_rows, 128), jnp.int32),
            pltpu.VMEM((1 + xt * xt, edge, edge), f32),
            pltpu.VMEM(lam_ladder.shape, bf16),
            pltpu.VMEM(lam_ladder.shape, bf16),
            pltpu.VMEM((n_vir, rows, edge), f32),
            pltpu.VMEM((n_vir - 1, rows, edge), f32),
            pltpu.VMEM((8, 128), jnp.int32),
            pltpu.VMEM((8, 128), jnp.int32),
            *per_chunk(blocks, 2 * owned),
            *per_chunk(blocks, 2 * owned),
            *per_chunk(owned),
            *per_chunk(owned),
            *per_chunk(owned),
            *per_chunk(2 * owned),
            sem((4,)),
            sem,
            sem((3, blocks)),
            sem((3, blocks)),
            sem((3,)),
            sem((3,)),
            sem((n_vir - 1,)),
            sem((n_vir - 1,)),
            sem,
            sem,
        ],
        compiler_params=pltpu.CompilerParams(
            collective_id=0, has_side_effects=True, vmem_limit_bytes=40 * 1024 * 1024
        ),
        cost_estimate=pl.CostEstimate(flops=10**9, bytes_accessed=4 * 10**6, transcendentals=0),
    )(cycle_left, cycle_right, cycle_dest, ladder_mask, partner_slot, t2_tiles, cycle_ints, lam_ladder, ladder_ints)
    return sym / denom


def solution(mesh):
    in_specs = (
        P("occ", "vir", None, None, None),
        P("occ", "vir", None, None, None),
        P("occ", "vir", None),
        P("occ", "vir", None),
        P("occ", "vir", None),
        P("occ", "vir"),
        P("vir", None),
        P("occ", "vir"),
        P("occ", None),
        P("occ", "vir"),
    )
    local = functools.partial(body, mesh.shape["occ"], mesh.shape["vir"])
    return jax.shard_map(local, mesh=mesh, in_specs=in_specs, out_specs=P("occ", "vir"), check_vma=False)
```

time: 159 us -> 38 us (0.24)
  waiting for transfers between devices: 73 us -> 0 us
  starting transfers between devices: 32.3 us -> 0 us
  Pallas kernels: 0 us -> 29.4 us
  between operations: 13.5 us -> 0.03 us
  matrix products: 11.9 us -> 0 us
  local copies, waits for them, and re-layouts: 17.3 us -> 7.47 us
  other arithmetic: 9.71 us -> 0.68 us
    all_to_all x2 -> x0, waiting for transfers between devices: 48.8 us -> none  [the longest x1 48.8 us: body(): lax.all_to_all(send_tiles, 'occ', split_axis=0, concat_axis=0, tiled=True)]
    pallas_call x0 -> x1, Pallas kernels: none -> 29.4 us  [body(): pl.pallas_call(functools.partial(kernel, n_occ, n_vir, chunks), out_shape...]
    ppermute x4 -> x0, starting transfers between devices: 16.8 us -> none  [partner_2(): lax.ppermute(array, axis, [(i, i ^ 1 << distance) for i in range(lax.axis...]
    all_to_all x2 -> x0, starting transfers between devices: 15.4 us -> none  [the longest x1 8.31 us: body(): lax.all_to_all(send_slots, 'occ', split_axis=0, concat_axis=0, tiled=True)]
    gather x10 -> x0, local copies, waits for them, and re-layouts: 15.2 us -> none  [the longest x3 4.97 us: task_block(): right_tiles[ridx]]
    ppermute x4 -> x0, waiting for transfers between devices: 13.8 us -> none  [partner_2(): lax.ppermute(array, axis, [(i, i ^ 1 << distance) for i in range(lax.axis...]
    dot_general x5 -> x0, matrix products: 11.9 us -> none  [the longest x3 5.86 us: task_block(): jnp.einsum('btk,bkc->btc', left_tiles[lidx], right_tiles[ridx], precision...]
    reduce_scatter x1 -> x0, waiting for transfers between devices: 10.3 us -> none  [body(): lax.psum_scatter(partial_ladder, 'vir', scatter_dimension=1, tiled=True)]
  transfers between devices with their start and end apart: 7 -> 0, of which waited for: 6 -> 0; matrix products, arithmetic and copies ran while one was open for 18% -> 0% of each run, Pallas kernels for 0% -> 0%
where the time goes in v1:
time: 38 us; the launch traced here: 37.6 us
  Pallas kernels  29.4 us (77%)
  local copies, waits for them, and re-layouts  7.47 us (20%)
  other arithmetic  0.68 us (2%)
    pallas_call x1, Pallas kernels, body(): pl.pallas_call(functools.partial(kernel, n_occ, n_vir, chunks), out_shape...  29.4 us
    unnamed x20, local copies, waits for them, and re-layouts  7.47 us

profile of v1, /device:TPU:0, one launch (start us, length us, event | category | flops | bytes accessed | tf_op | source)
XLA Modules:
  0.0 37.6 jit_solution(77167358019638387)
XLA Ops:
  0.0 0.0 copy-start
  0.0 1.0 %copy-done = f32[1,1,4,128,256]{4,3,2,1,0:T(8,128)S(1)} copy-done((f32[1,1,4,128,256]{4,3,2,1,0:T(8,128)S(1)}, f32[1,1,4,128,256]{4,3,2,1,0:T(8,128)}, u32[]{:S(2)}) %copy-start) | copy-done | bytes 524312
  1.0 0.0 copy-start.1
  1.0 1.0 %copy-done.1 = f32[1,1,4,256,128]{4,3,2,1,0:T(8,128)S(1)} copy-done((f32[1,1,4,256,128]{4,3,2,1,0:T(8,128)S(1)}, f32[1,1,4,256,128]{4,3,2,1,0:T(8,128)}, u32[]{:S(2)}) %copy-start.1) | copy-done | bytes 524312
  2.1 0.0 copy-start.2
  2.1 1.0 %copy-done.2 = f32[256,512]{1,0:T(8,128)S(1)} copy-done((f32[256,512]{1,0:T(8,128)S(1)}, f32[256,512]{1,0:T(8,128)}, u32[]{:S(2)}) %copy-start.2) | copy-done | bytes 524312
  3.1 0.0 copy-start.3
  3.1 1.0 %copy-done.3 = f32[512,256]{1,0:T(8,128)S(1)} copy-done((f32[512,256]{1,0:T(8,128)S(1)}, f32[512,256]{1,0:T(8,128)}, u32[]{:S(2)}) %copy-start.3) | copy-done | bytes 524312
  4.2 0.0 copy-start.4
  4.2 0.7 %copy-done.4 = s32[2,4]{1,0:T(2,128)S(1)} copy-done((s32[2,4]{1,0:T(2,128)S(1)}, s32[2,4]{1,0:T(2,128)}, u32[]{:S(2)}) %copy-start.4) | copy-done | bytes 56
  4.8 0.0 copy-start.5
  4.9 0.7 %copy-done.5 = s32[1,1,24]{2,1,0:T(1,128)S(1)} copy-done((s32[1,1,24]{2,1,0:T(1,128)S(1)}, s32[1,1,24]{2,1,0:T(1,128)}, u32[]{:S(2)}) %copy-start.5) | copy-done | bytes 120
  5.5 0.0 copy-start.6
  5.5 0.7 %copy-done.6 = s32[1,1,24]{2,1,0:T(1,128)S(1)} copy-done((s32[1,1,24]{2,1,0:T(1,128)S(1)}, s32[1,1,24]{2,1,0:T(1,128)}, u32[]{:S(2)}) %copy-start.6) | copy-done | bytes 120
  6.2 0.0 copy-start.7
  6.2 0.7 %copy-done.7 = s32[1,1,24]{2,1,0:T(1,128)S(1)} copy-done((s32[1,1,24]{2,1,0:T(1,128)S(1)}, s32[1,1,24]{2,1,0:T(1,128)}, u32[]{:S(2)}) %copy-start.7) | copy-done | bytes 120
  6.8 0.0 copy-start.8
  6.8 0.7 %copy-done.8 = s32[1,2]{1,0:T(1,128)S(1)} copy-done((s32[1,2]{1,0:T(1,128)S(1)}, s32[1,2]{1,0:T(1,128)}, u32[]{:S(2)}) %copy-start.8) | copy-done | bytes 32
  7.5 0.0 copy-start.9
  7.5 29.4 %shard_map.100 = f32[256,128]{1,0:T(8,128)S(1)} custom-call(s32[1,1,24]{2,1,0:T(1,128)S(1)} %copy-done.5, s32[1,1,24]{2,1,0:T(1,128)S(1)} %copy-done.6, s32[1,1,24]{2,1,0:T(1,128)S(1)} %copy-done.7, s32[2,4]{1,0:T(2,128)S(1)} %copy-done.4, s32[1,2]{1,0:T(1,128)S(1)} %copy-done.8, f32[1,1,4,128,256]{4,3,2,1,0:T(8,128)S(1)} %copy-done, ...), custom_call_target="tpu_custom_call" | custom-call | flops 1000000000 | bytes 4000000 | tf_op jit(solution)/shard_map/pallas_call | solution.py:273
  36.9 0.0 copy-done.9
  36.9 0.7 %div.3 = f32[256,128]{1,0:T(8,128)} divide(f32[256,128]{1,0:T(8,128)S(1)} %shard_map.100, f32[256,128]{1,0:T(8,128)S(1)} %copy-done.9) | non-fusion elementwise | flops 32768 | bytes 393216 | tf_op jit(solution)/shard_map/div | solution.py:314
Async XLA Ops:
  0.0 1.0 %copy-start = (f32[1,1,4,128,256]{4,3,2,1,0:T(8,128)S(1)}, f32[1,1,4,128,256]{4,3,2,1,0:T(8,128)}, u32[]{:S(2)}) copy-start(f32[1,1,4,128,256]{4,3,2,1,0:T(8,128)} %t2_hbm.1) | copy-start | bytes 1572868
  1.0 1.0 %copy-start.1 = (f32[1,1,4,256,128]{4,3,2,1,0:T(8,128)S(1)}, f32[1,1,4,256,128]{4,3,2,1,0:T(8,128)}, u32[]{:S(2)}) copy-start(f32[1,1,4,256,128]{4,3,2,1,0:T(8,128)} %ints_hbm.1) | copy-start | bytes 1572868
  2.1 1.0 %copy-start.2 = (f32[256,512]{1,0:T(8,128)S(1)}, f32[256,512]{1,0:T(8,128)}, u32[]{:S(2)}) copy-start(f32[256,512]{1,0:T(8,128)} %lam_hbm.1) | copy-start | bytes 1572868
  3.1 1.0 %copy-start.3 = (f32[512,256]{1,0:T(8,128)S(1)}, f32[512,256]{1,0:T(8,128)}, u32[]{:S(2)}) copy-start(f32[512,256]{1,0:T(8,128)} %lints_hbm.1) | copy-start | bytes 1572868
  4.2 0.7 %copy-start.4 = (s32[2,4]{1,0:T(2,128)S(1)}, s32[2,4]{1,0:T(2,128)}, u32[]{:S(2)}) copy-start(s32[2,4]{1,0:T(2,128)} %mask.1) | copy-start | bytes 100
  4.8 0.7 %copy-start.5 = (s32[1,1,24]{2,1,0:T(1,128)S(1)}, s32[1,1,24]{2,1,0:T(1,128)}, u32[]{:S(2)}) copy-start(s32[1,1,24]{2,1,0:T(1,128)} %left.1) | copy-start | bytes 292
  5.5 0.7 %copy-start.6 = (s32[1,1,24]{2,1,0:T(1,128)S(1)}, s32[1,1,24]{2,1,0:T(1,128)}, u32[]{:S(2)}) copy-start(s32[1,1,24]{2,1,0:T(1,128)} %right.1) | copy-start | bytes 292
  6.2 0.7 %copy-start.7 = (s32[1,1,24]{2,1,0:T(1,128)S(1)}, s32[1,1,24]{2,1,0:T(1,128)}, u32[]{:S(2)}) copy-start(s32[1,1,24]{2,1,0:T(1,128)} %dest.1) | copy-start | bytes 292
  6.8 0.7 %copy-start.8 = (s32[1,2]{1,0:T(1,128)S(1)}, s32[1,2]{1,0:T(1,128)}, u32[]{:S(2)}) copy-start(s32[1,2]{1,0:T(1,128)} %slot.1) | copy-start | bytes 28
  7.5 29.5 %copy-start.9 = (f32[256,128]{1,0:T(8,128)S(1)}, f32[256,128]{1,0:T(8,128)}, u32[]{:S(2)}) copy-start(f32[256,128]{1,0:T(8,128)} %param.19) | copy-start | bytes 393220

commit v2 on v1

--- a/solution.py
+++ b/solution.py
@@ -37,10 +37,28 @@
     return [(sum(sizes[:c]), sizes[c]) for c in range(3)]
 
 
+def turned(matrix, x):
+    return dot(matrix, x).astype(bf16)
+
+
+def split3(x):
+    hi, rest = split2(x)
+    mid, low = split2(x - hi.astype(f32))
+    return hi, mid, low
+
+
+def permutation(size, reverse):
+    row = lax.broadcasted_iota(jnp.int32, (size, size), 0)
+    col = lax.broadcasted_iota(jnp.int32, (size, size), 1)
+    target = row + reverse * (size - 1 - 2 * row)
+    return jnp.where(target == col, 1.0, 0.0).astype(bf16)
+
+
 def kernel(
     n_occ, n_vir, chunks,
-    left, right, dest, mask, slot, t2_hbm, ints_hbm, lam_hbm, lints_hbm,
+    left_hbm, right_hbm, dest_hbm, mask_hbm, slot_hbm, t2_hbm, ints_hbm, lam_hbm, lints_hbm,
     out,
+    left, right, dest, mask, slot,
     t2, ints, lam, lints, code_v, code_s, prod, lam_hi, lam_lo, lad, lad_got, flag, flag_got,
     c0, c1, c2, r0, r1, r2, s0, s1, s2, t0, t1, t2s, g0, g1, g2, w0, w1, w2,
     load_sem, code_sem, send_sem, recv_sem, fin_send, fin_recv, lad_send, lad_recv, flag_send, flag_recv,
@@ -48,12 +66,13 @@
     acc, got, own, fin, fin_got, flips = (c0, c1, c2), (r0, r1, r2), (s0, s1, s2), (t0, t1, t2s), (g0, g1, g2), (w0, w1, w2)
     edge = prod.shape[1]
     xt = t2.shape[0]
+    pairs = xt * xt
     owned = 2
     count = dest.shape[2]
     bits = n_occ.bit_length() - 1
     levels = bits - 1
     blocks = n_occ // 2
-    width = (xt * xt).bit_length()
+    width = pairs.bit_length()
     p = lax.axis_index("occ")
     q = lax.axis_index("vir")
     upper = p // blocks
@@ -64,7 +83,11 @@
     loads = [
         pltpu.make_async_copy(src, dst, load_sem.at[i])
         for i, (src, dst) in enumerate(
-            ((t2_hbm.at[0, 0], t2), (ints_hbm.at[0, 0], ints), (lam_hbm, lam), (lints_hbm, lints))
+            (
+                (left_hbm, left), (right_hbm, right), (dest_hbm, dest), (slot_hbm, slot),
+                (t2_hbm.at[0, 0], t2), (ints_hbm.at[0, 0], ints),
+                (mask_hbm, mask), (lam_hbm, lam), (lints_hbm, lints),
+            )
         )
     ]
     for load in loads:
@@ -80,6 +103,8 @@
     tile_id = lax.broadcasted_iota(jnp.int32, code_v.shape, 0) * 128 + lax.broadcasted_iota(
         jnp.int32, code_v.shape, 1
     )
+    for load in loads[:4]:
+        load.wait()
 
     def note(t, packed):
         code = left[0, 0, t] * xt + right[0, 0, t] + 1
@@ -89,17 +114,26 @@
     codes = pltpu.make_async_copy(code_v, code_s, code_sem)
     codes.start()
     flag[...] = jnp.full(flag.shape, slot[0, 0], jnp.int32)
+
     prod[0] = jnp.zeros((edge, edge), f32)
-
-    loads[0].wait()
-    loads[1].wait()
+    prod[1 + pairs] = jnp.zeros((edge, edge), f32)
+    turn = permutation(edge, 1)
+    loads[4].wait()
+    loads[5].wait()
     a = split2(t2[...].reshape(xt * edge, t2.shape[2]))
+    a_turned = [
+        jnp.concatenate([turned(turn, x[l * edge : (l + 1) * edge]) for l in range(xt)], axis=0) for x in a
+    ]
     for r in range(0, xt, 2):
-        b = split2(jnp.concatenate([ints[r], ints[r + 1]], axis=1))
-        res = dot3(a, b)
-        for l in range(xt):
-            for d in range(2):
-                prod[1 + l * xt + r + d] = res[l * edge : (l + 1) * edge, d * edge : (d + 1) * edge]
+        sides = [split2(ints[r + d]) for d in range(2)]
+        b = [jnp.concatenate([sides[0][k], sides[1][k]], axis=1) for k in range(2)]
+        b_turned = [
+            jnp.concatenate([turned(sides[0][k], turn), turned(sides[1][k], turn)], axis=1) for k in range(2)
+        ]
+        for base, res in ((1, dot3(a, b)), (2 + pairs, dot3(a_turned, b_turned))):
+            for l in range(xt):
+                for d in range(2):
+                    prod[base + l * xt + r + d] = res[l * edge : (l + 1) * edge, d * edge : (d + 1) * edge]
     codes.wait()
 
     def assemble(c, i):
@@ -107,14 +141,20 @@
         home = cls
         for h in range(levels):
             home = toggle(home, orders[c][h], (i // (1 << h)) % 2)
+        ids = []
         for j in range(2 * owned):
-            owner = home if j < owned else n_occ - 1 - home
-            g = owner * owned + j % owned
+            g = (home if j < owned else n_occ - 1 - home) * owned + j % owned
             packed = code_s[g // 128, g % 128]
-            ids = [lax.shift_right_logical(packed, width * k) & ((1 << width) - 1) for k in range(CAP)]
-            for at, row in ((0, lo), (half, edge - lo - half)):
-                tiles = [prod[k, row : row + half, :] for k in ids]
-                acc[c][i, j, at : at + half, :] = tiles[0] + tiles[1] + tiles[2]
+            base = 0 if j < owned else 1 + pairs
+            ids.append([base + (lax.shift_right_logical(packed, width * k) & ((1 << width) - 1)) for k in range(CAP)])
+        for at, row in ((0, lo), (half, edge - lo - half)):
+            low0, low1, up0, up1 = [
+                prod[k[0], row : row + half, :] + prod[k[1], row : row + half, :] + prod[k[2], row : row + half, :]
+                for k in ids
+            ]
+            acc[c][i, 0, at : at + half, :] = low0 + up0
+            acc[c][i, 1, at : at + half, :] = low0 + up1
+            acc[c][i, 2, at : at + half, :] = low1 + up0
 
     def step_copy(c, i, h):
         return pltpu.make_async_remote_copy(
@@ -127,11 +167,6 @@
         )
 
     pl.semaphore_wait(barrier, bits + n_vir - 1)
-    flag_copy = pltpu.make_async_remote_copy(
-        src_ref=flag, dst_ref=flag_got, send_sem=flag_send, recv_sem=flag_recv,
-        device_id=(partner, q), device_id_type=MESH,
-    )
-    flag_copy.start()
 
     top = blocks // 2
 
@@ -142,13 +177,19 @@
             assemble(c, i)
             step_copy(c, i, levels - 1).start()
 
+    flag_copy = pltpu.make_async_remote_copy(
+        src_ref=flag, dst_ref=flag_got, send_sem=flag_send, recv_sem=flag_recv,
+        device_id=(partner, q), device_id_type=MESH,
+    )
+    flag_copy.start()
+
     @pl.loop(0, top)
     def _(n):
         for c in range(3):
             assemble(c, top - 1 - n)
 
-    loads[2].wait()
-    loads[3].wait()
+    for load in loads[6:]:
+        load.wait()
     for s in range(owned):
         for b in range(mask.shape[1]):
             rows, cols = pl.ds(s * edge, edge), pl.ds(b * edge, edge)
@@ -173,6 +214,26 @@
         )
         lad_copies[-1].start()
     lad[0] = ladder(q)
+    lanes = permutation(edge, upper)
+
+    def add_ladder():
+        for copy in lad_copies:
+            copy.wait_recv()
+        total = lad[0]
+        for off in range(1, n_vir):
+            total = total + lad_got[off - 1]
+        for s in range(owned):
+            y = None
+            for piece in split3(total[s * edge : (s + 1) * edge]):
+                part = dot(lanes, turned(piece, lanes))
+                y = part if y is None else y + part
+            lad[0, s * edge : (s + 1) * edge, :] = y
+        for c in range(3):
+            lo, half = chunks[c]
+            for at, row in ((0, lo), (half, edge - lo - half)):
+                here = pl.ds(at, half)
+                for j, s in ((0, 0), (1, upper), (2, 1 - upper)):
+                    acc[c][0, j, here, :] = acc[c][0, j, here, :] + lad[0, pl.ds(pl.multiple_of(s * edge + row, 8), half), :]
 
     def take(c, i, h):
         for k in range(h, levels):
@@ -180,6 +241,8 @@
             acc[c][i] = acc[c][i] + got[c][i + (1 << k)]
 
     for h in reversed(range(levels - 1)):
+        if h == 0:
+            add_ladder()
 
         @pl.loop(0, 1 << h)
         def _(n):
@@ -188,15 +251,7 @@
                 take(c, i, h + 1)
                 step_copy(c, i, h).start()
 
-    for copy in lad_copies:
-        copy.wait_recv()
-    total = lad[0]
-    for off in range(1, n_vir):
-        total = total + lad_got[off - 1]
-    lad[0] = total
     flag_copy.wait_recv()
-    lanes = lax.broadcasted_iota(jnp.int32, (edge, edge), 0) + lax.broadcasted_iota(jnp.int32, (edge, edge), 1)
-    turn_lanes = jnp.where(lanes == edge - 1, 1.0, 0.0).astype(bf16)
 
     def fin_copy(c):
         return pltpu.make_async_remote_copy(
@@ -205,42 +260,29 @@
         )
 
     for c in range(3):
-        lo, half = chunks[c]
-        m = 2 * half
+        m = 2 * chunks[c][1]
         take(c, 0, 0)
-        for s in range(owned):
-            j = upper * owned + s
-            for at, row in ((0, lo), (half, edge - lo - half)):
-                here = pl.ds(at, half)
-                acc[c][0, j, here, :] = acc[c][0, j, here, :] + lad[0, s * edge + row : s * edge + row + half, :]
-        x = acc[c][0].reshape(4 * m, edge)
-        hi, rest = split2(x)
-        mid, low = split2(x - hi.astype(f32))
-        size = 4 * m
-        rows = lax.broadcasted_iota(jnp.int32, (size, size), 0) + lax.broadcasted_iota(jnp.int32, (size, size), 1)
-        turn_rows = jnp.where(rows == size - 1, 1.0, 0.0).astype(bf16)
-        y = None
-        for piece in (hi, mid, low):
-            part = dot(turn_rows, dot(piece, turn_lanes).astype(bf16))
-            y = part if y is None else y + part
-        flips[c][...] = y.reshape(4, m, edge)
         for target, which, swap in ((fin[c], 1 - upper, flag_got), (own[c], upper, flag)):
-            first = flips[c][2 * which + 1]
-            second = flips[c][2 * which]
             keep = jnp.broadcast_to(swap[0:1, :] == 0, (m, edge))
-            target[0] = acc[c][0, 2 * which] + jnp.where(keep, first, second)
-            target[1] = acc[c][0, 2 * which + 1] + jnp.where(keep, second, first)
+            first, second = acc[c][0, 1 + which], acc[c][0, 2 - which]
+            target[0] = jnp.where(keep, acc[c][0, 0], first)
+            target[1] = jnp.where(keep, (first - acc[c][0, 0]) + second, second)
             if target is fin[c]:
                 fin_copy(c).start()
 
     for c in range(3):
         lo, half = chunks[c]
+        size = 2 * owned * half
+        rows = permutation(size, upper)
         fin_copy(c).wait_recv()
+        y = None
+        for piece in split3((own[c][...] + fin_got[c][...]).reshape(size, edge)):
+            part = dot(rows, turned(piece, lanes))
+            y = part if y is None else y + part
+        flips[c][...] = y.reshape(owned, 2 * half, edge)
         for s in range(owned):
             for at, row in ((0, lo), (half, edge - lo - half)):
-                out[s * edge + row : s * edge + row + half, :] = (
-                    own[c][s, at : at + half, :] + fin_got[c][s, at : at + half, :]
-                )
+                out[s * edge + row : s * edge + row + half, :] = flips[c][s + upper * (1 - 2 * s), at : at + half, :]
 
     flag_copy.wait_send()
     for copy in lad_copies:
@@ -268,34 +310,39 @@
     rows = owned * edge
     per_chunk = lambda *lead: [pltpu.VMEM((*lead, 2 * half, edge), f32) for _, half in chunks]
     sem = pltpu.SemaphoreType.DMA
-    smem = pl.BlockSpec(memory_space=pltpu.SMEM)
-    hbm = pl.BlockSpec(memory_space=pl.ANY)
+    hbm = pl.BlockSpec(memory_space=pltpu.HBM)
+    smem = lambda x: pltpu.SMEM(x.shape, x.dtype)
     sym = pl.pallas_call(
         functools.partial(kernel, n_occ, n_vir, chunks),
         out_shape=jax.ShapeDtypeStruct((rows, edge), f32),
-        in_specs=[smem] * 5 + [hbm] * 4,
+        in_specs=[hbm] * 9,
         out_specs=pl.BlockSpec(memory_space=pltpu.VMEM),
         scratch_shapes=[
+            smem(cycle_left),
+            smem(cycle_right),
+            smem(cycle_dest),
+            smem(ladder_mask),
+            smem(partner_slot),
             pltpu.VMEM((xt, edge, kc), f32),
             pltpu.VMEM((xt, kc, edge), f32),
             pltpu.VMEM(lam_ladder.shape, f32),
             pltpu.VMEM(ladder_ints.shape, f32),
             pltpu.VMEM((code_rows, 128), jnp.int32),
             pltpu.SMEM((code_rows, 128), jnp.int32),
-            pltpu.VMEM((1 + xt * xt, edge, edge), f32),
+            pltpu.VMEM((2 + 2 * xt * xt, edge, edge), f32),
             pltpu.VMEM(lam_ladder.shape, bf16),
             pltpu.VMEM(lam_ladder.shape, bf16),
             pltpu.VMEM((n_vir, rows, edge), f32),
             pltpu.VMEM((n_vir - 1, rows, edge), f32),
             pltpu.VMEM((8, 128), jnp.int32),
             pltpu.VMEM((8, 128), jnp.int32),
-            *per_chunk(blocks, 2 * owned),
-            *per_chunk(blocks, 2 * owned),
+            *per_chunk(blocks, 3),
+            *per_chunk(blocks, 3),
             *per_chunk(owned),
             *per_chunk(owned),
             *per_chunk(owned),
-            *per_chunk(2 * owned),
-            sem((4,)),
+            *per_chunk(owned),
+            sem((9,)),
             sem,
             sem((3, blocks)),
             sem((3, blocks)),
@@ -307,7 +354,7 @@
             sem,
         ],
         compiler_params=pltpu.CompilerParams(
-            collective_id=0, has_side_effects=True, vmem_limit_bytes=40 * 1024 * 1024
+            collective_id=0, has_side_effects=True, vmem_limit_bytes=62 * 1024 * 1024
         ),
         cost_estimate=pl.CostEstimate(flops=10**9, bytes_accessed=4 * 10**6, transcendentals=0),
     )(cycle_left, cycle_right, cycle_dest, ladder_mask, partner_slot, t2_tiles, cycle_ints, lam_ladder, ladder_ints)

time: 38 us -> 29 us (0.76)
  local copies, waits for them, and re-layouts: 7.47 us -> 0.01 us
  Pallas kernels: 29.4 us -> 27.2 us
  other arithmetic: 0.68 us -> 1.58 us
    unnamed x20 -> x2, local copies, waits for them, and re-layouts: 7.47 us -> 0.01 us
    pallas_call x1, Pallas kernels: 29.4 us -> 27.2 us  [body(): pl.pallas_call(functools.partial(kernel, n_occ, n_vir, chunks), out_shape...]
    div x1, other arithmetic: 0.68 us -> 1.58 us  [body(): return sym / denom]
where the time goes in v2:
time: 29 us; the launch traced here: 28.8 us
  Pallas kernels  27.2 us (94%)
  other arithmetic  1.58 us (5%)
    pallas_call x1, Pallas kernels, body(): pl.pallas_call(functools.partial(kernel, n_occ, n_vir, chunks), out_shape...  27.2 us
    div x1, other arithmetic, body(): return sym / denom  1.58 us

profile of v2, /device:TPU:0, one launch (start us, length us, event | category | flops | bytes accessed | tf_op | source)
XLA Modules:
  0.0 28.8 jit_solution(9371970988383903914)
XLA Ops:
  0.0 0.0 copy-start
  0.0 27.2 %shard_map.100 = f32[256,128]{1,0:T(8,128)} custom-call(s32[1,1,24]{2,1,0:T(1,128)} %left_hbm.1, s32[1,1,24]{2,1,0:T(1,128)} %right_hbm.1, s32[1,1,24]{2,1,0:T(1,128)} %dest_hbm.1, s32[2,4]{1,0:T(2,128)} %mask_hbm.1, s32[1,2]{1,0:T(1,128)} %slot_hbm.1, f32[1,1,4,128,256]{4,3,2,1,0:T(8,128)} %t2_hbm.1, f32[1,1,4,256,128]{4,3,2,1,0:T(8,128)} %ints_hbm.1, ...), custom_call_target="tpu_custom_call" | custom-call | flops 1000000000 | bytes 4000000 | tf_op jit(solution)/shard_map/pallas_call | solution.py:315
  27.2 0.0 copy-done
  27.2 1.6 %div.3 = f32[256,128]{1,0:T(8,128)} divide(f32[256,128]{1,0:T(8,128)} %shard_map.100, f32[256,128]{1,0:T(8,128)S(1)} %copy-done) | non-fusion elementwise | flops 32768 | bytes 393216 | tf_op jit(solution)/shard_map/div | solution.py:361
Async XLA Ops:
  0.0 27.2 %copy-start = (f32[256,128]{1,0:T(8,128)S(1)}, f32[256,128]{1,0:T(8,128)}, u32[]{:S(2)}) copy-start(f32[256,128]{1,0:T(8,128)} %param.19) | copy-start | bytes 393220

commit v3 on v2

--- a/solution.py
+++ b/solution.py
@@ -30,11 +30,13 @@
     return value + on * bit * (1 - 2 * ((value // bit) % 2))
 
 
+CHUNKS = 6
+AXES = 3
+
+
 def chunk_plan(edge):
-    unit = edge // 2 // 8
-    big = unit // 3 + unit % 3 // 2
-    sizes = [big * 8, big * 8, (unit - 2 * big) * 8]
-    return [(sum(sizes[:c]), sizes[c]) for c in range(3)]
+    sizes = [units * (edge // 16) for units in (2, 2, 1, 1, 1, 1)]
+    return [(sum(sizes[:c]), sizes[c]) for c in range(CHUNKS)]
 
 
 def turned(matrix, x):
@@ -60,10 +62,10 @@
     out,
     left, right, dest, mask, slot,
     t2, ints, lam, lints, code_v, code_s, prod, lam_hi, lam_lo, lad, lad_got, flag, flag_got,
-    c0, c1, c2, r0, r1, r2, s0, s1, s2, t0, t1, t2s, g0, g1, g2, w0, w1, w2,
+    per_chunk,
     load_sem, code_sem, send_sem, recv_sem, fin_send, fin_recv, lad_send, lad_recv, flag_send, flag_recv,
 ):
-    acc, got, own, fin, fin_got, flips = (c0, c1, c2), (r0, r1, r2), (s0, s1, s2), (t0, t1, t2s), (g0, g1, g2), (w0, w1, w2)
+    acc, got, own, fin, fin_got, flips = per_chunk
     edge = prod.shape[1]
     xt = t2.shape[0]
     pairs = xt * xt
@@ -78,7 +80,8 @@
     upper = p // blocks
     cls = p + upper * (n_occ - 1 - 2 * p)
     partner = n_occ - 1 - p
-    orders = [[1 << ((c + levels - 1 - h) % levels) for h in range(levels)] for c in range(3)]
+    orders = [[1 << ((c % AXES + levels - 1 - h) % levels) for h in range(levels)] for c in range(CHUNKS)]
+    early, late = range(AXES), range(AXES, CHUNKS)
 
     loads = [
         pltpu.make_async_copy(src, dst, load_sem.at[i])
@@ -173,7 +176,7 @@
     @pl.loop(0, top)
     def _(n):
         i = blocks - 1 - n
-        for c in range(3):
+        for c in early:
             assemble(c, i)
             step_copy(c, i, levels - 1).start()
 
@@ -185,8 +188,13 @@
 
     @pl.loop(0, top)
     def _(n):
-        for c in range(3):
+        for c in early:
             assemble(c, top - 1 - n)
+
+    @pl.loop(0, blocks)
+    def _(n):
+        for c in late:
+            assemble(c, n)
 
     for load in loads[6:]:
         load.wait()
@@ -228,7 +236,7 @@
                 part = dot(lanes, turned(piece, lanes))
                 y = part if y is None else y + part
             lad[0, s * edge : (s + 1) * edge, :] = y
-        for c in range(3):
+        for c in range(CHUNKS):
             lo, half = chunks[c]
             for at, row in ((0, lo), (half, edge - lo - half)):
                 here = pl.ds(at, half)
@@ -240,26 +248,13 @@
             step_copy(c, i + (1 << k), k).wait_recv()
             acc[c][i] = acc[c][i] + got[c][i + (1 << k)]
 
-    for h in reversed(range(levels - 1)):
-        if h == 0:
-            add_ladder()
-
-        @pl.loop(0, 1 << h)
-        def _(n):
-            i = 2 * (1 << h) - 1 - n
-            for c in range(3):
-                take(c, i, h + 1)
-                step_copy(c, i, h).start()
-
-    flag_copy.wait_recv()
-
     def fin_copy(c):
         return pltpu.make_async_remote_copy(
             src_ref=fin[c], dst_ref=fin_got[c], send_sem=fin_send.at[c], recv_sem=fin_recv.at[c],
             device_id=(partner, q), device_id_type=MESH,
         )
 
-    for c in range(3):
+    def finish(c):
         m = 2 * chunks[c][1]
         take(c, 0, 0)
         for target, which, swap in ((fin[c], 1 - upper, flag_got), (own[c], upper, flag)):
@@ -270,7 +265,34 @@
             if target is fin[c]:
                 fin_copy(c).start()
 
-    for c in range(3):
+    for n in range(top):
+        for c in late:
+            step_copy(c, blocks - 1 - n, levels - 1).start()
+        i = top - 1 - n
+        if i > 0:
+            h = i.bit_length() - 1
+            for c in early:
+                take(c, i, h + 1)
+                step_copy(c, i, h).start()
+
+    add_ladder()
+    flag_copy.wait_recv()
+    for c in early:
+        finish(c)
+
+    for h in reversed(range(levels - 1)):
+
+        @pl.loop(0, 1 << h)
+        def _(n):
+            i = 2 * (1 << h) - 1 - n
+            for c in late:
+                take(c, i, h + 1)
+                step_copy(c, i, h).start()
+
+    for c in late:
+        finish(c)
+
+    for c in range(CHUNKS):
         lo, half = chunks[c]
         size = 2 * owned * half
         rows = permutation(size, upper)
@@ -287,7 +309,7 @@
     flag_copy.wait_send()
     for copy in lad_copies:
         copy.wait_send()
-    for c in range(3):
+    for c in range(CHUNKS):
         fin_copy(c).wait_send()
         for h in range(levels):
 
@@ -308,13 +330,13 @@
     tiles = n_occ * owned
     code_rows = -(-tiles // 128)
     rows = owned * edge
-    per_chunk = lambda *lead: [pltpu.VMEM((*lead, 2 * half, edge), f32) for _, half in chunks]
+    per_chunk = lambda *lead: tuple(pltpu.VMEM((*lead, 2 * half, edge), f32) for _, half in chunks)
     sem = pltpu.SemaphoreType.DMA
     hbm = pl.BlockSpec(memory_space=pltpu.HBM)
     smem = lambda x: pltpu.SMEM(x.shape, x.dtype)
     sym = pl.pallas_call(
         functools.partial(kernel, n_occ, n_vir, chunks),
-        out_shape=jax.ShapeDtypeStruct((rows, edge), f32),
+        out_shape=pltpu.VMEM((rows, edge), f32),
         in_specs=[hbm] * 9,
         out_specs=pl.BlockSpec(memory_space=pltpu.VMEM),
         scratch_shapes=[
@@ -336,25 +358,23 @@
             pltpu.VMEM((n_vir - 1, rows, edge), f32),
             pltpu.VMEM((8, 128), jnp.int32),
             pltpu.VMEM((8, 128), jnp.int32),
-            *per_chunk(blocks, 3),
-            *per_chunk(blocks, 3),
-            *per_chunk(owned),
-            *per_chunk(owned),
-            *per_chunk(owned),
-            *per_chunk(owned),
+            (
+                per_chunk(blocks, 3), per_chunk(blocks, 3),
+                per_chunk(owned), per_chunk(owned), per_chunk(owned), per_chunk(owned),
+            ),
             sem((9,)),
             sem,
-            sem((3, blocks)),
-            sem((3, blocks)),
-            sem((3,)),
-            sem((3,)),
+            sem((CHUNKS, blocks)),
+            sem((CHUNKS, blocks)),
+            sem((CHUNKS,)),
+            sem((CHUNKS,)),
             sem((n_vir - 1,)),
             sem((n_vir - 1,)),
             sem,
             sem,
         ],
         compiler_params=pltpu.CompilerParams(
-            collective_id=0, has_side_effects=True, vmem_limit_bytes=62 * 1024 * 1024
+            collective_id=0, has_side_effects=True, vmem_limit_bytes=56 * 1024 * 1024
         ),
         cost_estimate=pl.CostEstimate(flops=10**9, bytes_accessed=4 * 10**6, transcendentals=0),
     )(cycle_left, cycle_right, cycle_dest, ladder_mask, partner_slot, t2_tiles, cycle_ints, lam_ladder, ladder_ints)

time: 29 us -> 32 us (1.10)
  Pallas kernels: 27.2 us -> 31.1 us
  other arithmetic: 1.58 us -> 0.68 us
    pallas_call x1, Pallas kernels: 27.2 us -> 31.1 us  [body(): pl.pallas_call(functools.partial(kernel, n_occ, n_vir, chunks), out_shape...]
    div x1, other arithmetic: 1.58 us -> 0.68 us  [body(): return sym / denom]
where the time goes in v3:
time: 32 us; the launch traced here: 31.9 us
  Pallas kernels  31.1 us (97%)
  other arithmetic  0.68 us (2%)
    pallas_call x1, Pallas kernels, body(): pl.pallas_call(functools.partial(kernel, n_occ, n_vir, chunks), out_shape...  31.1 us
    div x1, other arithmetic, body(): return sym / denom  0.68 us

profile of v3, /device:TPU:0, one launch (start us, length us, event | category | flops | bytes accessed | tf_op | source)
XLA Modules:
  0.0 31.9 jit_solution(11223896283642275135)
XLA Ops:
  0.0 0.0 copy-start
  0.0 31.1 %shard_map.100 = f32[256,128]{1,0:T(8,128)S(1)} custom-call(s32[1,1,24]{2,1,0:T(1,128)} %left_hbm.1, s32[1,1,24]{2,1,0:T(1,128)} %right_hbm.1, s32[1,1,24]{2,1,0:T(1,128)} %dest_hbm.1, s32[2,4]{1,0:T(2,128)} %mask_hbm.1, s32[1,2]{1,0:T(1,128)} %slot_hbm.1, f32[1,1,4,128,256]{4,3,2,1,0:T(8,128)} %t2_hbm.1, f32[1,1,4,256,128]{4,3,2,1,0:T(8,128)} %ints_hbm.1, ...), custom_call_target="tpu_custom_call" | custom-call | flops 1000000000 | bytes 4000000 | tf_op jit(solution)/shard_map/pallas_call | solution.py:337
  31.2 0.0 copy-done
  31.2 0.7 %div.3 = f32[256,128]{1,0:T(8,128)} divide(f32[256,128]{1,0:T(8,128)S(1)} %shard_map.100, f32[256,128]{1,0:T(8,128)S(1)} %copy-done) | non-fusion elementwise | flops 32768 | bytes 393216 | tf_op jit(solution)/shard_map/div | solution.py:381
Async XLA Ops:
  0.0 31.2 %copy-start = (f32[256,128]{1,0:T(8,128)S(1)}, f32[256,128]{1,0:T(8,128)}, u32[]{:S(2)}) copy-start(f32[256,128]{1,0:T(8,128)} %param.19) | copy-start | bytes 393220

commit v4 on v3

--- a/solution.py
+++ b/solution.py
@@ -26,16 +26,11 @@
     return dot(a[0], b[0]) + (dot(a[0], b[1]) + dot(a[1], b[0]))
 
 
-def toggle(value, bit, on=1):
-    return value + on * bit * (1 - 2 * ((value // bit) % 2))
-
-
-CHUNKS = 6
-AXES = 3
+CHUNKS = 3
 
 
 def chunk_plan(edge):
-    sizes = [units * (edge // 16) for units in (2, 2, 1, 1, 1, 1)]
+    sizes = [units * (edge // 16) for units in (3, 3, 2)]
     return [(sum(sizes[:c]), sizes[c]) for c in range(CHUNKS)]
 
 
@@ -77,11 +72,13 @@
     width = pairs.bit_length()
     p = lax.axis_index("occ")
     q = lax.axis_index("vir")
-    upper = p // blocks
+    upper = lax.div(p, blocks)
     cls = p + upper * (n_occ - 1 - 2 * p)
     partner = n_occ - 1 - p
-    orders = [[1 << ((c % AXES + levels - 1 - h) % levels) for h in range(levels)] for c in range(CHUNKS)]
-    early, late = range(AXES), range(AXES, CHUNKS)
+    orders = [[1 << ((c + levels - 1 - h) % levels) for h in range(levels)] for c in range(CHUNKS)]
+    offsets = {1 << b: (1 << b) * (1 - 2 * lax.rem(lax.div(p, 1 << b), 2)) for b in range(levels)}
+    peers = {bit: p + offset for bit, offset in offsets.items()}
+    turns = {bit: offset * (1 - 2 * upper) for bit, offset in offsets.items()}
 
     loads = [
         pltpu.make_async_copy(src, dst, load_sem.at[i])
@@ -97,11 +94,11 @@
         load.start()
 
     barrier = pltpu.get_barrier_semaphore()
-    for b in range(levels):
-        pl.semaphore_signal(barrier, inc=1, device_id=(toggle(p, 1 << b), q), device_id_type=MESH)
+    for peer in peers.values():
+        pl.semaphore_signal(barrier, inc=1, device_id=(peer, q), device_id_type=MESH)
     pl.semaphore_signal(barrier, inc=1, device_id=(partner, q), device_id_type=MESH)
     for off in range(1, n_vir):
-        pl.semaphore_signal(barrier, inc=1, device_id=(p, (q + off) % n_vir), device_id_type=MESH)
+        pl.semaphore_signal(barrier, inc=1, device_id=(p, lax.rem(q + off, n_vir)), device_id_type=MESH)
 
     tile_id = lax.broadcasted_iota(jnp.int32, code_v.shape, 0) * 128 + lax.broadcasted_iota(
         jnp.int32, code_v.shape, 1
@@ -113,7 +110,7 @@
         code = left[0, 0, t] * xt + right[0, 0, t] + 1
         return jnp.where(tile_id == dest[0, 0, t], packed * (1 << width) + code, packed)
 
-    code_v[...] = lax.fori_loop(0, count, note, jnp.zeros(code_v.shape, jnp.int32))
+    code_v[...] = lax.fori_loop(0, count, note, jnp.zeros(code_v.shape, jnp.int32), unroll=8)
     codes = pltpu.make_async_copy(code_v, code_s, code_sem)
     codes.start()
     flag[...] = jnp.full(flag.shape, slot[0, 0], jnp.int32)
@@ -139,25 +136,33 @@
                     prod[base + l * xt + r + d] = res[l * edge : (l + 1) * edge, d * edge : (d + 1) * edge]
     codes.wait()
 
-    def assemble(c, i):
-        lo, half = chunks[c]
+    def place(c, rel):
+        return sum(1 << h for h in range(levels) if rel & orders[c][h])
+
+    def assemble(rel):
         home = cls
-        for h in range(levels):
-            home = toggle(home, orders[c][h], (i // (1 << h)) % 2)
+        for bit in turns:
+            if rel & bit:
+                home = home + turns[bit]
         ids = []
         for j in range(2 * owned):
             g = (home if j < owned else n_occ - 1 - home) * owned + j % owned
-            packed = code_s[g // 128, g % 128]
+            packed = code_s[0, g] if code_s.shape[0] == 1 else code_s[lax.div(g, 128), lax.rem(g, 128)]
             base = 0 if j < owned else 1 + pairs
             ids.append([base + (lax.shift_right_logical(packed, width * k) & ((1 << width) - 1)) for k in range(CAP)])
-        for at, row in ((0, lo), (half, edge - lo - half)):
-            low0, low1, up0, up1 = [
-                prod[k[0], row : row + half, :] + prod[k[1], row : row + half, :] + prod[k[2], row : row + half, :]
-                for k in ids
-            ]
-            acc[c][i, 0, at : at + half, :] = low0 + up0
-            acc[c][i, 1, at : at + half, :] = low0 + up1
-            acc[c][i, 2, at : at + half, :] = low1 + up0
+        for c in range(CHUNKS):
+            lo, half = chunks[c]
+            i = place(c, rel)
+            for at, row in ((0, lo), (half, edge - lo - half)):
+                low0, low1, up0, up1 = [
+                    prod[k[0], row : row + half, :] + prod[k[1], row : row + half, :] + prod[k[2], row : row + half, :]
+                    for k in ids
+                ]
+                acc[c][i, 0, at : at + half, :] = low0 + up0
+                acc[c][i, 1, at : at + half, :] = low0 + up1
+                acc[c][i, 2, at : at + half, :] = low1 + up0
+            if i >= blocks // 2:
+                step_copy(c, i, levels - 1).start()
 
     def step_copy(c, i, h):
         return pltpu.make_async_remote_copy(
@@ -165,36 +170,20 @@
             dst_ref=got[c].at[i],
             send_sem=send_sem.at[c, i],
             recv_sem=recv_sem.at[c, i],
-            device_id=(toggle(p, orders[c][h]), q),
+            device_id=(peers[orders[c][h]], q),
             device_id_type=MESH,
         )
 
     pl.semaphore_wait(barrier, bits + n_vir - 1)
 
-    top = blocks // 2
-
-    @pl.loop(0, top)
-    def _(n):
-        i = blocks - 1 - n
-        for c in early:
-            assemble(c, i)
-            step_copy(c, i, levels - 1).start()
+    for rel in sorted(range(blocks), key=lambda r: -sum(r >> b & 1 for b in range(levels))):
+        assemble(rel)
 
     flag_copy = pltpu.make_async_remote_copy(
         src_ref=flag, dst_ref=flag_got, send_sem=flag_send, recv_sem=flag_recv,
         device_id=(partner, q), device_id_type=MESH,
     )
     flag_copy.start()
-
-    @pl.loop(0, top)
-    def _(n):
-        for c in early:
-            assemble(c, top - 1 - n)
-
-    @pl.loop(0, blocks)
-    def _(n):
-        for c in late:
-            assemble(c, n)
 
     for load in loads[6:]:
         load.wait()
@@ -211,7 +200,7 @@
 
     lad_copies = []
     for off in range(1, n_vir):
-        column = (q + off) % n_vir
+        column = lax.rem(q + off, n_vir)
         lad[off] = ladder(column)
         lad_copies.append(
             pltpu.make_async_remote_copy(
@@ -265,31 +254,16 @@
             if target is fin[c]:
                 fin_copy(c).start()
 
-    for n in range(top):
-        for c in late:
-            step_copy(c, blocks - 1 - n, levels - 1).start()
-        i = top - 1 - n
-        if i > 0:
-            h = i.bit_length() - 1
-            for c in early:
+    for h in reversed(range(levels - 1)):
+        if h == 0:
+            add_ladder()
+        for i in reversed(range(1 << h, 2 << h)):
+            for c in range(CHUNKS):
                 take(c, i, h + 1)
                 step_copy(c, i, h).start()
 
-    add_ladder()
     flag_copy.wait_recv()
-    for c in early:
-        finish(c)
-
-    for h in reversed(range(levels - 1)):
-
-        @pl.loop(0, 1 << h)
-        def _(n):
-            i = 2 * (1 << h) - 1 - n
-            for c in late:
-                take(c, i, h + 1)
-                step_copy(c, i, h).start()
-
-    for c in late:
+    for c in range(CHUNKS):
         finish(c)
 
     for c in range(CHUNKS):

time: 32 us -> 27.3 us (0.85)
  Pallas kernels: 31.1 us -> 26.5 us
    pallas_call x1, Pallas kernels: 31.1 us -> 26.5 us  [body(): pl.pallas_call(functools.partial(kernel, n_occ, n_vir, chunks), out_shape...]
where the time goes in v4:
time: 27.3 us; the launch traced here: 27.2 us
  Pallas kernels  26.5 us (97%)
  other arithmetic  0.68 us (2%)
    pallas_call x1, Pallas kernels, body(): pl.pallas_call(functools.partial(kernel, n_occ, n_vir, chunks), out_shape...  26.5 us
    div x1, other arithmetic, body(): return sym / denom  0.68 us

profile of v4, /device:TPU:0, one launch (start us, length us, event | category | flops | bytes accessed | tf_op | source)
XLA Modules:
  0.0 27.2 jit_solution(400229616656552115)
XLA Ops:
  0.0 0.0 copy-start
  0.0 26.5 %shard_map.100 = f32[256,128]{1,0:T(8,128)S(1)} custom-call(s32[1,1,24]{2,1,0:T(1,128)} %left_hbm.1, s32[1,1,24]{2,1,0:T(1,128)} %right_hbm.1, s32[1,1,24]{2,1,0:T(1,128)} %dest_hbm.1, s32[2,4]{1,0:T(2,128)} %mask_hbm.1, s32[1,2]{1,0:T(1,128)} %slot_hbm.1, f32[1,1,4,128,256]{4,3,2,1,0:T(8,128)} %t2_hbm.1, f32[1,1,4,256,128]{4,3,2,1,0:T(8,128)} %ints_hbm.1, ...), custom_call_target="tpu_custom_call" | custom-call | flops 1000000000 | bytes 4000000 | tf_op jit(solution)/shard_map/pallas_call | solution.py:311
  26.5 0.0 copy-done
  26.5 0.7 %div.3 = f32[256,128]{1,0:T(8,128)} divide(f32[256,128]{1,0:T(8,128)S(1)} %shard_map.100, f32[256,128]{1,0:T(8,128)S(1)} %copy-done) | non-fusion elementwise | flops 32768 | bytes 393216 | tf_op jit(solution)/shard_map/div | solution.py:355
Async XLA Ops:
  0.0 26.5 %copy-start = (f32[256,128]{1,0:T(8,128)S(1)}, f32[256,128]{1,0:T(8,128)}, u32[]{:S(2)}) copy-start(f32[256,128]{1,0:T(8,128)} %param.19) | copy-start | bytes 393220

commit v5 on v4

--- a/solution.py
+++ b/solution.py
@@ -26,11 +26,12 @@
     return dot(a[0], b[0]) + (dot(a[0], b[1]) + dot(a[1], b[0]))
 
 
-CHUNKS = 3
+CHUNKS = 6
+AXES = 3
 
 
 def chunk_plan(edge):
-    sizes = [units * (edge // 16) for units in (3, 3, 2)]
+    sizes = [units * (edge // 16) for units in (2, 2, 1, 1, 1, 1)]
     return [(sum(sizes[:c]), sizes[c]) for c in range(CHUNKS)]
 
 
@@ -75,7 +76,11 @@
     upper = lax.div(p, blocks)
     cls = p + upper * (n_occ - 1 - 2 * p)
     partner = n_occ - 1 - p
-    orders = [[1 << ((c + levels - 1 - h) % levels) for h in range(levels)] for c in range(CHUNKS)]
+    orders = [[1 << ((c % AXES + levels - 1 - h) % levels) for h in range(levels)] for c in range(CHUNKS)]
+    early, late = range(AXES), range(AXES, CHUNKS)
+    low, high = levels - 1, levels
+    pieces = [(1 << h, 2 << h, h) for h in range(levels - 1)]
+    pieces += [(blocks // 2, 3 * blocks // 4, levels - 1), (3 * blocks // 4, blocks, levels - 1)]
     offsets = {1 << b: (1 << b) * (1 - 2 * lax.rem(lax.div(p, 1 << b), 2)) for b in range(levels)}
     peers = {bit: p + offset for bit, offset in offsets.items()}
     turns = {bit: offset * (1 - 2 * upper) for bit, offset in offsets.items()}
@@ -161,23 +166,32 @@
                 acc[c][i, 0, at : at + half, :] = low0 + up0
                 acc[c][i, 1, at : at + half, :] = low0 + up1
                 acc[c][i, 2, at : at + half, :] = low1 + up0
-            if i >= blocks // 2:
-                step_copy(c, i, levels - 1).start()
-
-    def step_copy(c, i, h):
+
+    def step_copy(c, n):
+        start, stop, h = pieces[n]
         return pltpu.make_async_remote_copy(
-            src_ref=acc[c].at[i],
-            dst_ref=got[c].at[i],
-            send_sem=send_sem.at[c, i],
-            recv_sem=recv_sem.at[c, i],
+            src_ref=acc[c].at[pl.ds(start, stop - start)],
+            dst_ref=got[c].at[pl.ds(start, stop - start)],
+            send_sem=send_sem.at[c, n],
+            recv_sem=recv_sem.at[c, n],
             device_id=(peers[orders[c][h]], q),
             device_id_type=MESH,
         )
 
     pl.semaphore_wait(barrier, bits + n_vir - 1)
 
-    for rel in sorted(range(blocks), key=lambda r: -sum(r >> b & 1 for b in range(levels))):
+    rels = sorted(range(blocks), key=lambda r: -sum(r >> b & 1 for b in range(levels)))
+    done, sent = set(), set()
+    for rel in rels:
         assemble(rel)
+        done.add(rel)
+        for n, group in ((high, early), (low, early), (high, late), (low, late)):
+            start, stop, _ = pieces[n]
+            held = [r for r in range(blocks) for c in group if start <= place(c, r) < stop]
+            if (n, group) not in sent and done.issuperset(held) and (group is early or (low, early) in sent):
+                sent.add((n, group))
+                for c in group:
+                    step_copy(c, n).start()
 
     flag_copy = pltpu.make_async_remote_copy(
         src_ref=flag, dst_ref=flag_got, send_sem=flag_send, recv_sem=flag_recv,
@@ -232,10 +246,17 @@
                 for j, s in ((0, 0), (1, upper), (2, 1 - upper)):
                     acc[c][0, j, here, :] = acc[c][0, j, here, :] + lad[0, pl.ds(pl.multiple_of(s * edge + row, 8), half), :]
 
-    def take(c, i, h):
-        for k in range(h, levels):
-            step_copy(c, i + (1 << k), k).wait_recv()
-            acc[c][i] = acc[c][i] + got[c][i + (1 << k)]
+    arrived = set()
+
+    def take(c, start, stop):
+        for k in reversed(range(levels)):
+            if 1 << k < stop:
+                continue
+            n = k if k < low else high if start >= blocks // 4 else low
+            if (c, n) not in arrived:
+                arrived.add((c, n))
+                step_copy(c, n).wait_recv()
+            acc[c][start:stop] = acc[c][start:stop] + got[c][start + (1 << k) : stop + (1 << k)]
 
     def fin_copy(c):
         return pltpu.make_async_remote_copy(
@@ -245,7 +266,7 @@
 
     def finish(c):
         m = 2 * chunks[c][1]
-        take(c, 0, 0)
+        take(c, 0, 1)
         for target, which, swap in ((fin[c], 1 - upper, flag_got), (own[c], upper, flag)):
             keep = jnp.broadcast_to(swap[0:1, :] == 0, (m, edge))
             first, second = acc[c][0, 1 + which], acc[c][0, 2 - which]
@@ -254,17 +275,16 @@
             if target is fin[c]:
                 fin_copy(c).start()
 
-    for h in reversed(range(levels - 1)):
-        if h == 0:
+    for group in (early, late):
+        for h in reversed(range(levels - 1)):
+            for c in group:
+                take(c, 1 << h, 2 << h)
+                step_copy(c, h).start()
+        if group is early:
             add_ladder()
-        for i in reversed(range(1 << h, 2 << h)):
-            for c in range(CHUNKS):
-                take(c, i, h + 1)
-                step_copy(c, i, h).start()
-
-    flag_copy.wait_recv()
-    for c in range(CHUNKS):
-        finish(c)
+            flag_copy.wait_recv()
+        for c in group:
+            finish(c)
 
     for c in range(CHUNKS):
         lo, half = chunks[c]
@@ -285,11 +305,8 @@
         copy.wait_send()
     for c in range(CHUNKS):
         fin_copy(c).wait_send()
-        for h in range(levels):
-
-            @pl.loop(1 << h, 2 << h)
-            def _(i):
-                step_copy(c, i, h).wait_send()
+        for n in range(len(pieces)):
+            step_copy(c, n).wait_send()
 
 
 def body(
@@ -338,8 +355,8 @@
             ),
             sem((9,)),
             sem,
-            sem((CHUNKS, blocks)),
-            sem((CHUNKS, blocks)),
+            sem((CHUNKS, n_occ.bit_length())),
+            sem((CHUNKS, n_occ.bit_length())),
             sem((CHUNKS,)),
             sem((CHUNKS,)),
             sem((n_vir - 1,)),

time: 27.3 us -> 34.9 us (1.28)
  Pallas kernels: 26.5 us -> 34 us
    pallas_call x1, Pallas kernels: 26.5 us -> 34 us  [body(): pl.pallas_call(functools.partial(kernel, n_occ, n_vir, chunks), out_shape...]
where the time goes in v5:
time: 34.9 us; the launch traced here: 34.7 us
  Pallas kernels  34 us (97%)
  other arithmetic  0.68 us (2%)
    pallas_call x1, Pallas kernels, body(): pl.pallas_call(functools.partial(kernel, n_occ, n_vir, chunks), out_shape...  34 us

profile of v5, /device:TPU:0, one launch (start us, length us, event | category | flops | bytes accessed | tf_op | source)
XLA Modules:
  0.0 34.7 jit_solution(9480428170917919123)
XLA Ops:
  0.0 0.0 copy-start
  0.0 34.0 %shard_map.100 = f32[256,128]{1,0:T(8,128)S(1)} custom-call(s32[1,1,24]{2,1,0:T(1,128)} %left_hbm.1, s32[1,1,24]{2,1,0:T(1,128)} %right_hbm.1, s32[1,1,24]{2,1,0:T(1,128)} %dest_hbm.1, s32[2,4]{1,0:T(2,128)} %mask_hbm.1, s32[1,2]{1,0:T(1,128)} %slot_hbm.1, f32[1,1,4,128,256]{4,3,2,1,0:T(8,128)} %t2_hbm.1, f32[1,1,4,256,128]{4,3,2,1,0:T(8,128)} %ints_hbm.1, ...), custom_call_target="tpu_custom_call" | custom-call | flops 1000000000 | bytes 4000000 | tf_op jit(solution)/shard_map/pallas_call | solution.py:328
  34.0 0.0 copy-done
  34.1 0.7 %div.3 = f32[256,128]{1,0:T(8,128)} divide(f32[256,128]{1,0:T(8,128)S(1)} %shard_map.100, f32[256,128]{1,0:T(8,128)S(1)} %copy-done) | non-fusion elementwise | flops 32768 | bytes 393216 | tf_op jit(solution)/shard_map/div | solution.py:372
Async XLA Ops:
  0.0 34.0 %copy-start = (f32[256,128]{1,0:T(8,128)S(1)}, f32[256,128]{1,0:T(8,128)}, u32[]{:S(2)}) copy-start(f32[256,128]{1,0:T(8,128)} %param.19) | copy-start | bytes 393220

commit v6 on v4

--- a/solution.py
+++ b/solution.py
@@ -60,7 +60,7 @@
     per_chunk,
     load_sem, code_sem, send_sem, recv_sem, fin_send, fin_recv, lad_send, lad_recv, flag_send, flag_recv,
 ):
-    acc, got, own, fin, fin_got, flips = per_chunk
+    acc, got, own, fin, fin_got = per_chunk
     edge = prod.shape[1]
     xt = t2.shape[0]
     pairs = xt * xt
@@ -269,16 +269,27 @@
     for c in range(CHUNKS):
         lo, half = chunks[c]
         size = 2 * owned * half
-        rows = permutation(size, upper)
+        rows = permutation(size, 1)
         fin_copy(c).wait_recv()
-        y = None
-        for piece in split3((own[c][...] + fin_got[c][...]).reshape(size, edge)):
-            part = dot(rows, turned(piece, lanes))
-            y = part if y is None else y + part
-        flips[c][...] = y.reshape(owned, 2 * half, edge)
-        for s in range(owned):
-            for at, row in ((0, lo), (half, edge - lo - half)):
-                out[s * edge + row : s * edge + row + half, :] = flips[c][s + upper * (1 - 2 * s), at : at + half, :]
+
+        @pl.when(upper == 0)
+        def _():
+            for s in range(owned):
+                for at, row in ((0, lo), (half, edge - lo - half)):
+                    out[s * edge + row : s * edge + row + half, :] = (
+                        own[c][s, at : at + half, :] + fin_got[c][s, at : at + half, :]
+                    )
+
+        @pl.when(upper == 1)
+        def _():
+            y = None
+            for piece in split3((own[c][...] + fin_got[c][...]).reshape(size, edge)):
+                part = dot(rows, turned(piece, turn))
+                y = part if y is None else y + part
+            y = y.reshape(owned, 2 * half, edge)
+            for s in range(owned):
+                for at, row in ((0, lo), (half, edge - lo - half)):
+                    out[s * edge + row : s * edge + row + half, :] = y[owned - 1 - s, at : at + half, :]
 
     flag_copy.wait_send()
     for copy in lad_copies:
@@ -334,7 +345,7 @@
             pltpu.VMEM((8, 128), jnp.int32),
             (
                 per_chunk(blocks, 3), per_chunk(blocks, 3),
-                per_chunk(owned), per_chunk(owned), per_chunk(owned), per_chunk(owned),
+                per_chunk(owned), per_chunk(owned), per_chunk(owned),
             ),
             sem((9,)),
             sem,

time: 27.3 us -> 27 us (0.989)
  Pallas kernels: 26.5 us -> 26.2 us
where the time goes in v6:
time: 27 us; the launch traced here: 26.9 us
  Pallas kernels  26.2 us (97%)
  other arithmetic  0.68 us (3%)
    pallas_call x1, Pallas kernels, body(): pl.pallas_call(functools.partial(kernel, n_occ, n_vir, chunks), out_shape...  26.2 us
    div x1, other arithmetic, body(): return sym / denom  0.68 us

profile of v6, /device:TPU:0, one launch (start us, length us, event | category | flops | bytes accessed | tf_op | source)
XLA Modules:
  0.0 26.9 jit_solution(1009491458998820585)
XLA Ops:
  0.0 0.0 copy-start
  0.0 26.2 %shard_map.100 = f32[256,128]{1,0:T(8,128)S(1)} custom-call(s32[1,1,24]{2,1,0:T(1,128)} %left_hbm.1, s32[1,1,24]{2,1,0:T(1,128)} %right_hbm.1, s32[1,1,24]{2,1,0:T(1,128)} %dest_hbm.1, s32[2,4]{1,0:T(2,128)} %mask_hbm.1, s32[1,2]{1,0:T(1,128)} %slot_hbm.1, f32[1,1,4,128,256]{4,3,2,1,0:T(8,128)} %t2_hbm.1, f32[1,1,4,256,128]{4,3,2,1,0:T(8,128)} %ints_hbm.1, ...), custom_call_target="tpu_custom_call" | custom-call | flops 1000000000 | bytes 4000000 | tf_op jit(solution)/shard_map/pallas_call | solution.py:322
  26.2 0.0 copy-done
  26.2 0.7 %div.3 = f32[256,128]{1,0:T(8,128)} divide(f32[256,128]{1,0:T(8,128)S(1)} %shard_map.100, f32[256,128]{1,0:T(8,128)S(1)} %copy-done) | non-fusion elementwise | flops 32768 | bytes 393216 | tf_op jit(solution)/shard_map/div | solution.py:366
Async XLA Ops:
  0.0 26.2 %copy-start = (f32[256,128]{1,0:T(8,128)S(1)}, f32[256,128]{1,0:T(8,128)}, u32[]{:S(2)}) copy-start(f32[256,128]{1,0:T(8,128)} %param.19) | copy-start | bytes 393220
